TPU v7x, 256 devices: a whole 4x4x8 slice. The times are simulated.
256 devices in a mesh: depth: 4 (over x_lo, core), row: 16 (over z, x_hi), col: 4 (over y).
Axes of the slice: x: 4 (x_hi: 2, x_lo: 2; x = x_hi * 2 + x_lo), y: 4, z: 8, core: 2. Of those that a mesh axis runs over, the one named last changes fastest.
Arguments:
- alignment: bfloat16 [512, 512, 256], P('depth', ('row', 'col')), may hold values from -6 to 6
- seq_mask: int32 [512], replicated, may hold values 0 or 1
- residue_mask: int32 [512], replicated, may hold values 0 or 1
- layer_norm_gain: float32 [256], replicated, may hold values from 0.5 to 1.5
- layer_norm_bias: float32 [256], replicated, may hold values from -3 to 3
- left_projection_weight: bfloat16 [256, 32], replicated, may hold values from -0.375 to 0.375
- left_bias: float32 [32], replicated, may hold values from -3 to 3
- right_projection_weight: bfloat16 [256, 32], replicated, may hold values from -0.375 to 0.375
- right_bias: float32 [32], replicated, may hold values from -3 to 3
- out_weight: bfloat16 [1024, 128], replicated, may hold values from -0.1875 to 0.1875
- pair_grad: bfloat16 [512, 512, 128], P('row', 'col'), may hold values from -6 to 6
Outputs:
- alignment_grad: bfloat16 [512, 512, 256], P('depth', ('row', 'col'))
- left_weight_grad: float32 [256, 32], replicated
- left_bias_grad: float32 [32], replicated
- right_weight_grad: float32 [256, 32], replicated
- right_bias_grad: float32 [32], replicated
- norm_gain_grad: float32 [256], replicated
- norm_bias_grad: float32 [256], replicated
- out_weight_grad: float32 [1024, 128], replicated
All inputs are finite; a program needn't handle non-finite values.
Results may differ from a plain program's by a relative error of at most 0.022.
Values may be sent and summed in bfloat16 or wider, within the bound.
A program may use at most 64 MiB of HBM per device.

v0:
```python
import math

import jax
import jax.numpy as jnp
from jax import lax
from jax.sharding import PartitionSpec as P


def layer_norm(alignment, layer_norm_gain, layer_norm_bias):
    values = alignment.astype(jnp.float32)
    centred = values - jnp.mean(values, axis=-1, keepdims=True)
    inv_std = lax.rsqrt(jnp.mean(centred * centred, axis=-1, keepdims=True) + 1e-05)
    unit_values = centred * inv_std
    normed = (unit_values * layer_norm_gain + layer_norm_bias).astype(jnp.bfloat16)
    return (unit_values, inv_std, normed)


def project(normed, weight, bias, cell_mask):
    linear = jnp.einsum("srm,mc->src", normed, weight, preferred_element_type=jnp.float32) + bias
    return (linear * cell_mask[:, :, None]).astype(jnp.bfloat16)


def sectioned_sums(right_sum, total_res, row_index, col_index, row_block, col_block):
    local_sequences, chans = (right_sum.shape[1], right_sum.shape[2])
    empty_full = jnp.zeros((total_res, local_sequences, chans), jnp.float32)
    col_total = lax.psum(right_sum.astype(jnp.bfloat16), "row").astype(jnp.float32)
    padded = lax.dynamic_update_slice_in_dim(empty_full, col_total, col_index * col_block, 0)
    band = lax.dynamic_slice_in_dim(padded, row_index * row_block, row_block, 0)
    return lax.psum_scatter(
        band.astype(jnp.bfloat16), "col", scatter_dimension=0, tiled=True
    ).astype(jnp.float32)


def body(
    alignment,
    seq_mask,
    residue_mask,
    layer_norm_gain,
    layer_norm_bias,
    left_projection_weight,
    left_bias,
    right_projection_weight,
    right_bias,
    out_weight,
    pair_grad,
):
    local_sequences, local_residues, alignment_width = alignment.shape
    chans = left_projection_weight.shape[1]
    row_block, col_block, pair_width = pair_grad.shape
    total_res = residue_mask.shape[0]
    col_count = lax.axis_size("col")
    depth_index = lax.axis_index("depth")
    row_index = lax.axis_index("row")
    col_index = lax.axis_index("col")
    seq_float = seq_mask.astype(jnp.float32)
    res_float = residue_mask.astype(jnp.float32)
    seq_count = jnp.sum(seq_float)
    my_seqs = lax.dynamic_slice_in_dim(seq_float, depth_index * local_sequences, local_sequences)
    own_first = (row_index * col_count + col_index) * local_residues
    my_res = lax.dynamic_slice_in_dim(res_float, own_first, local_residues)
    cell_mask = my_seqs[:, None] * my_res[None, :]
    unit_values, inv_std, normed = layer_norm(alignment, layer_norm_gain, layer_norm_bias)
    left = project(normed, left_projection_weight, left_bias, cell_mask)
    right = project(normed, right_projection_weight, right_bias, cell_mask)
    left_own = jnp.transpose(left, (1, 0, 2))
    right_own = jnp.transpose(right, (1, 0, 2))
    left_rows = lax.all_gather(left_own, "col", axis=0, tiled=True)
    right_every = lax.all_gather(right_own, ("row", "col"), axis=0, tiled=True)
    right_cols = lax.dynamic_slice_in_dim(right_every, col_index * col_block, col_block, 0)
    first_res = lax.dynamic_slice_in_dim(res_float, row_index * row_block, row_block)
    second_res = lax.dynamic_slice_in_dim(res_float, col_index * col_block, col_block)
    divisor = jnp.maximum(seq_count * first_res[:, None] * second_res[None, :], 1.0)
    scaled = (pair_grad.astype(jnp.float32) / divisor[:, :, None]).astype(jnp.bfloat16)
    step_rows = math.gcd(row_block, 8)

    def one_block(running, pieces):
        out_grad, right_grad = running
        block_left, scaled_rows = pieces
        outer = jnp.einsum(
            "isc,jsd->ijcd", block_left, right_cols, preferred_element_type=jnp.float32
        ).astype(jnp.bfloat16)
        outer_flat = outer.reshape(-1, chans * chans)
        scaled_flat = scaled_rows.reshape(-1, pair_width)
        out_grad = out_grad + jnp.dot(outer_flat.T, scaled_flat, preferred_element_type=jnp.float32)
        outer_grad = jnp.dot(scaled_flat, out_weight.T, preferred_element_type=jnp.float32).astype(
            jnp.bfloat16
        )
        outer_grad = outer_grad.reshape(step_rows, col_block, chans, chans)
        rows_grad = jnp.einsum(
            "ijcd,jsd->isc", outer_grad, right_cols, preferred_element_type=jnp.float32
        )
        right_grad = right_grad + jnp.einsum(
            "ijcd,isc->jsd", outer_grad, block_left, preferred_element_type=jnp.float32
        )
        return ((out_grad, right_grad), rows_grad)

    start_state = (
        jnp.zeros((chans * chans, pair_width), jnp.float32),
        jnp.zeros((col_block, local_sequences, chans), jnp.float32),
    )
    blocks_in = (
        left_rows.reshape(row_block // step_rows, step_rows, local_sequences, chans),
        scaled.reshape(row_block // step_rows, step_rows, col_block, pair_width),
    )
    (out_weight_part, right_sum), left_parts = lax.scan(one_block, start_state, blocks_in)
    left_rows_grad = left_parts.reshape(row_block, local_sequences, chans)
    left_own_grad = lax.psum_scatter(
        left_rows_grad.astype(jnp.bfloat16), "col", scatter_dimension=0, tiled=True
    ).astype(jnp.float32)
    right_own_grad = sectioned_sums(
        right_sum, total_res, row_index, col_index, row_block, col_block
    )
    left_pre_grad = (jnp.transpose(left_own_grad, (1, 0, 2)) * cell_mask[:, :, None]).astype(
        jnp.bfloat16
    )
    right_pre_grad = (jnp.transpose(right_own_grad, (1, 0, 2)) * cell_mask[:, :, None]).astype(
        jnp.bfloat16
    )
    normed_grad = jnp.einsum(
        "src,mc->srm", left_pre_grad, left_projection_weight, preferred_element_type=jnp.float32
    )
    normed_grad = normed_grad + jnp.einsum(
        "src,mc->srm", right_pre_grad, right_projection_weight, preferred_element_type=jnp.float32
    )
    left_weight_part = jnp.einsum(
        "srm,src->mc", normed, left_pre_grad, preferred_element_type=jnp.float32
    )
    right_weight_part = jnp.einsum(
        "srm,src->mc", normed, right_pre_grad, preferred_element_type=jnp.float32
    )
    left_bias_part = jnp.sum(left_pre_grad.astype(jnp.float32), axis=(0, 1))
    right_bias_part = jnp.sum(right_pre_grad.astype(jnp.float32), axis=(0, 1))
    gain_part = jnp.sum(normed_grad * unit_values, axis=(0, 1))
    shift_part = jnp.sum(normed_grad, axis=(0, 1))
    weighted = normed_grad * layer_norm_gain
    alignment_grad = (
        inv_std
        * (
            weighted
            - jnp.mean(weighted, axis=-1, keepdims=True)
            - unit_values * jnp.mean(weighted * unit_values, axis=-1, keepdims=True)
        )
    ).astype(jnp.bfloat16)
    totals = lax.psum(
        (
            out_weight_part,
            left_weight_part,
            left_bias_part,
            right_weight_part,
            right_bias_part,
            gain_part,
            shift_part,
        ),
        ("depth", "row", "col"),
    )
    return (
        alignment_grad,
        totals[1],
        totals[2],
        totals[3],
        totals[4],
        totals[5],
        totals[6],
        totals[0],
    )


def solution(mesh):
    placed = (
        P("depth", ("row", "col"), None),
        P(),
        P(),
        P(),
        P(),
        P(),
        P(),
        P(),
        P(),
        P(),
        P("row", "col", None),
    )
    return jax.shard_map(
        body,
        mesh=mesh,
        in_specs=placed,
        out_specs=(P("depth", ("row", "col"), None), P(), P(), P(), P(), P(), P(), P()),
        check_vma=False,
    )
```

profile of v0, /device:TPU:1, one launch (start us, length us, event | category | flops | bytes accessed | tf_op | source)
XLA Modules:
  0.0 941.6 jit_solution(1939998848687308861)
XLA Ops:
  7.3 1.4 convert_reduce_fusion
  8.7 1.4 fusion.37
  11.7 2.2 fusion.29
  14.6 11.2 %all_gather.6 = bf16[32,128,32]{1,2,0:T(8,128)(2,1)S(1)} all-gather(bf16[8,128,32]{1,2,0:T(8,128)(2,1)S(1)} %fusion.28), channel_id=1, replica_groups=mesh['depth'=4,'row'=16,'col'=4] {'col'}, dimensions={0}, use_global_device_ids=true | all-gather | bytes 327680 | tf_op jit(solution)/shard_map/all_gather | solution.py:67
  26.4 0.7 dynamic-slice_multiply_fusion
  27.2 1.8 divide_convert_fusion
  29.0 113.4 %all-gather.2.cloned.1.call-done = bf16[512,128,32]{1,2,0:T(8,128)(2,1)} async-done(((bf16[8,128,32]{1,2,0:T(8,128)(2,1)}), bf16[512,128,32]{1,2,0:T(8,128)(2,1)}) %all-gather.2.cloned.1.call-update) | async-done | bytes 4194320 | tf_op jit(solution)/shard_map/all_gather | solution.py:68
  142.4 1.3 constant_dynamic-slice_fusion.1
  144.1 59.5 %while.15 = (s32[]{:T(128)}, f32[1024,128]{1,0:T(8,128)}, f32[128,128,32]{0,1,2:T(8,128)}, bf16[4,8,128,32]{2,3,1,0:T(8,128)(2,1)}, bf16[4,8,128,32]{2,3,1,0:T(8...) while((s32[]{:T(128)}, f32[1024,128]{1,0:T(8,128)}, ...), condition=%wide.region_4.5_spmd.clone, body=%wide.region_3.4_spmd.clone.sunk | while | flops 1345585152 | bytes 60358988 | solution.py:105
  144.2 0.9 copy-done.4
  145.9 1.4 copy.94
  147.3 1.5 fusion.78
  148.8 0.7 convolution_convert_fusion.2
  149.5 2.6 copy.95
  152.1 2.4 copy.96
  154.5 1.7 bitcast_add_fusion.2
  156.2 0.7 convolution_bitcast_fusion.4
  158.2 1.0 copy-done.4
  159.3 0.7 convert_bitcast_fusion.2
  160.0 1.4 copy.94
  161.3 2.6 fusion.78
  164.0 0.7 convolution_convert_fusion.2
  164.7 2.6 copy.95
  167.3 2.4 copy.96
  169.6 1.7 bitcast_add_fusion.2
  171.3 0.7 convolution_bitcast_fusion.4
  173.3 1.0 copy-done.4
  174.4 0.7 convert_bitcast_fusion.2
  175.1 1.4 copy.94
  176.5 2.6 fusion.78
  179.1 0.7 convolution_convert_fusion.2
  179.8 2.6 copy.95
  182.4 2.4 copy.96
  184.8 1.7 bitcast_add_fusion.2
  186.4 0.7 convolution_bitcast_fusion.4
  188.5 1.0 copy-done.4
  189.5 0.7 convert_bitcast_fusion.2
  190.2 1.4 copy.94
  191.6 2.6 fusion.78
  194.2 0.7 convolution_convert_fusion.2
  194.9 2.6 copy.95
  197.5 2.4 copy.96
  199.9 1.7 bitcast_add_fusion.2
  201.6 0.7 convolution_bitcast_fusion.4
  203.6 3.0 copy.46
  207.4 149.4 %all-reduce.5.cloned.1.call-done = bf16[128,128,32]{1,2,0:T(8,128)(2,1)} async-done(((bf16[128,128,32]{1,2,0:T(8,128)(2,1)}), bf16[128,128,32]{1,2,0:T(8,128)(2,1)}) %all-reduce.5.cloned.1.call-update) | async-done | bytes 1048592 | tf_op jit(solution)/shard_map/psum | solution.py:26
  358.1 0.7 dynamic-slice_convert_fusion
  359.7 29.6 %reduce-scatter.3.cloned.1.call-done = bf16[8,128,32]{1,2,0:T(8,128)(2,1)} async-done(((bf16[32,128,32]{1,2,0:T(8,128)(2,1)}), bf16[8,128,32]{1,2,0:T(8,128)(2,1)}) %reduce-scatter.3.cloned.1.call-update) | async-done | bytes 65552 | tf_op jit(solution)/shard_map/reduce_scatter | solution.py:107
  389.3 1.2 fusion.41
  390.5 1.9 convolution_bitcast_fusion.2
  392.4 22.2 %reduce-scatter.5.cloned.1.call-done = bf16[8,128,32]{1,2,0:T(8,128)(2,1)} async-done(((bf16[32,128,32]{1,2,0:T(8,128)(2,1)}), bf16[8,128,32]{1,2,0:T(8,128)(2,1)}) %reduce-scatter.5.cloned.1.call-update) | async-done | bytes 65552 | tf_op jit(solution)/shard_map/reduce_scatter | solution.py:29
  414.6 2.0 convolution_bitcast_fusion.1
  416.6 2.4 fusion.36
  419.7 0.7 fusion.35
  420.5 1.1 copy.47
  421.5 252.3 %all-reduce.7.cloned.1.call-done = f32[1024,128]{1,0:T(8,128)} async-done(((f32[1024,128]{1,0:T(8,128)}), f32[1024,128]{1,0:T(8,128)}) %all-reduce.7.cloned.1.call-update) | async-done | bytes 524304 | tf_op jit(solution)/shard_map/psum | solution.py:144
  673.9 251.6 %all-reduce.9.cloned.1.call-done = (f32[256,32]{0,1:T(8,128)}, f32[32]{0:T(128)}, f32[256,32]{0,1:T(8,128)}, f32[32]{0:T(128)}, f32[256]{0:T(256)}, /*index=5*/f32[256]{0:T(256)}) async-done(((f32[256,32]{0,1:T(8,128)}, f32[32]{0:T(128)}, f32[256,32]{0,1:T(8,128)}, f32[32]{0:T(128)}, f32[256]{0:T(256)}, /*index=5*/f32[256]{0:T(256)}), (f32[256,32]{0,1:T(8,128)}, f32[32]{0:T(128)}, f32[256,32]{0,1:T(8,128)}, ...) | async-done | bytes 67856 | tf_op jit(solution)/shard_map/psum | solution.py:144
  925.5 1.4 copy.119
  926.8 1.1 copy.120
  928.0 1.4 copy.121
  929.3 1.1 copy.122
  930.4 1.2 copy.123
  931.7 1.2 copy.124
  932.9 1.9 copy.125
  (115 shorter events, 13.2 us)
Async XLA Ops:
  7.2 4.5 copy-start
  7.2 6.9 copy-start.6
  7.2 6.9 copy-start.15
  7.2 6.9 copy-start.16
  7.2 6.9 copy-start.17
  7.2 6.9 copy-start.13
  7.2 135.2 %all-gather.2.cloned.1.call-start = ((), (), s32[]{:S(2)}) async-start(), calls=%async_computation.2 | async-start | bytes 4259840 | tf_op jit(solution)/shard_map/all_gather | solution.py:68
  10.1 15.7 %copy-start.14 = (s32[512]{0:T(512)S(1)}, s32[512]{0:T(512)}, u32[]{:S(2)}) copy-start(s32[512]{0:T(512)} %param.14) | copy-start | bytes 6148
  13.9 342.9 %all-reduce.5.cloned.1.call-start = ((), (), s32[]{:S(2)}) async-start(), calls=%async_computation.4 | async-start | bytes 2097152 | tf_op jit(solution)/shard_map/psum | solution.py:26
  144.1 1.0 copy-start.4
  144.1 1.1 copy-start.8
  147.3 1.5 copy-start.3
  152.1 2.4 copy-start.1
  152.1 2.4 copy-start.9
  156.2 1.4 copy-start.2
  156.2 2.0 copy-start.5
  158.2 1.0 copy-start.4
  158.2 1.1 copy-start.8
  161.3 2.6 copy-start.3
  167.2 2.4 copy-start.1
  167.3 2.4 copy-start.9
  171.3 1.4 copy-start.2
  171.3 2.0 copy-start.5
  173.3 1.0 copy-start.4
  173.3 1.1 copy-start.8
  176.5 2.6 copy-start.3
  182.4 2.4 copy-start.1
  182.4 2.4 copy-start.9
  186.4 1.4 copy-start.2
  186.4 2.0 copy-start.5
  188.4 1.0 copy-start.4
  188.4 1.1 copy-start.8
  191.6 2.6 copy-start.3
  197.5 2.4 copy-start.1
  197.5 2.4 copy-start.9
  201.6 1.4 copy-start.2
  201.6 2.0 copy-start.5
  206.6 182.7 %reduce-scatter.3.cloned.1.call-start = ((), (), s32[]{:S(2)}) async-start(), calls=%async_computation.3 | async-start | bytes 327680 | tf_op jit(solution)/shard_map/reduce_scatter | solution.py:107
  207.3 207.3 %reduce-scatter.5.cloned.1.call-start = ((), (), s32[]{:S(2)}) async-start(), calls=%async_computation.5 | async-start | bytes 327680 | tf_op jit(solution)/shard_map/reduce_scatter | solution.py:29
  356.8 1.2 copy-start.10
  358.0 32.5 %copy-start.7 = (bf16[128,8,256]{2,1,0:T(8,128)(2,1)S(1)}, bf16[128,8,256]{2,1,0:T(8,128)(2,1)}, u32[]{:S(2)}) copy-start(bf16[128,8,256]{2,1,0:T(8,128)(2,1)} %param.13) | copy-start | bytes 1572868
  358.9 315.0 %all-reduce.7.cloned.1.call-start = ((), (), s32[]{:S(2)}) async-start(), calls=%async_computation.6 | async-start | bytes 1048576 | tf_op jit(solution)/shard_map/psum | solution.py:144
  359.5 566.0 %all-reduce.9.cloned.1.call-start = ((), (), s32[]{:S(2)}) async-start(), calls=%async_computation.7 | async-start | bytes 137216 | tf_op jit(solution)/shard_map/psum | solution.py:144
  392.4 26.6 %copy-start.11 = (bf16[8,128,32]{1,2,0:T(8,128)(2,1)S(1)}, bf16[8,128,32]{1,2,0:T(8,128)(2,1)}, u32[]{:S(2)}) copy-start(bf16[8,128,32]{1,2,0:T(8,128)(2,1)} %reduce-scatter.3.cloned.1.call-done) | copy-start | bytes 196612
  414.6 4.4 copy-start.12
Sparse Core Ops, SparseCore 0:
  14.0 128.3 all-gather.1
  206.7 150.0 all-reduce.4
  360.0 29.2 reduce-scatter.2
  391.7 22.8 reduce-scatter.4
  421.4 252.4 all-reduce.6
  681.9 243.5 all-reduce.8
where the time goes:
time: 943 us; the launch traced here: 942 us
  waiting for transfers between devices  820 us (87%)
  local copies, waits for them, and re-layouts  51.9 us (6%)
  matrix products  34.6 us (4%)
  between operations  14.3 us (2%)
  blocking collectives  11.2 us (1%)
    psum x2, waiting for transfers between devices, body(): lax.psum((out_weight_part, left_weight_part, left_bias_part, right_weight...  504 us
    psum x1, waiting for transfers between devices, sectioned_sums(): lax.psum(right_sum.astype(jnp.bfloat16), 'row').astype(jnp.float32)  149 us
    all_gather x1, waiting for transfers between devices, body(): right_every = lax.all_gather(right_own, ('row', 'col'), axis=0, tiled=True)  113 us
    reduce_scatter x1, waiting for transfers between devices, body(): lax.psum_scatter(left_rows_grad.astype(jnp.bfloat16), 'col', scatter_dime...  29.6 us
    reduce_scatter x1, waiting for transfers between devices, sectioned_sums(): lax.psum_scatter(band.astype(jnp.bfloat16), 'col', scatter_dimension=0, t...  22.2 us
  transfers between devices with their start and end apart: 6, of which 6 were waited for; matrix products, arithmetic and copies ran while one was open for 2% of the time, Pallas kernels for 0%

commit v1 on v0

v1 whole, which is shorter than its diff:
```python
import jax
import jax.numpy as jnp
from jax import lax
from jax.experimental import pallas as pl
from jax.experimental.pallas import tpu as pltpu
from jax.sharding import PartitionSpec as P

F32, BF16 = jnp.float32, jnp.bfloat16
MESH = pl.DeviceIdType.MESH
NT = (((1,), (1,)), ((), ()))
TN = (((0,), (0,)), ((), ()))
PAIR, LEFT, RIGHT, RSUM, LSUM, W1, W2, W3, W4, W5, S1, S2, S3, S4 = range(14)


def dot(a, b):
    return jnp.dot(a, b, preferred_element_type=F32)


def dot_nt(a, b, **kw):
    return lax.dot_general(a, b, NT, preferred_element_type=F32, **kw)


def main_kernel(
    x_ref, seq_ref, res_ref, res_s, gain_ref, shift_ref, wl_ref, lb_ref, wr_ref, rb_ref, ow_ref, pair_ref,
    ag_ref, small_ref, wg_ref,
    inv1, xf, unit, norm, istd, ngrad, wt, bias, wf, wp, ps, scb, bd, og, outer, lb, lt, rf, rbuf, rt,
    rss, rsr, lss, lsr, lsf, wga, wgs, wgr, w1f, w2s, w2r, w3, w5, wgt, extra, sm, s1, s2, s3, sf,
    send_sem, recv_sem, local_sem,
):
    depth, row, col = lax.axis_index("depth"), lax.axis_index("row"), lax.axis_index("col")
    z, h = lax.div(row, 2), lax.rem(row, 2)
    q = h * 4 + col

    def zpeer(k):
        t = lax.rem(z + k, 8)
        return t, (depth, t * 2 + h, col)

    def qpeer(k):
        t = lax.rem(q + k, 8)
        return t, (depth, z * 2 + lax.div(t, 4), lax.rem(t, 4))

    def dpeer(k):
        t = lax.rem(depth + k, 4)
        return t, (t, row, col)

    def copy(which, k, src, dst, device):
        return pltpu.make_async_remote_copy(
            src_ref=src, dst_ref=dst, send_sem=send_sem.at[which, k], recv_sem=recv_sem.at[which, k],
            device_id=device, device_id_type=MESH,
        )

    def pair_copy(k):
        t, device = qpeer(k)
        return copy(PAIR, k, ps.at[t], scb.at[col, pl.ds(h * 32, 32)], device)

    def left_copy(k):
        block = lb.at[pl.ds(pl.multiple_of(q * 256, 256), 256)]
        return copy(LEFT, k, block, block, qpeer(k)[1])

    def right_copy(k):
        return copy(RIGHT, k, rbuf.at[z], rbuf.at[z], zpeer(k)[1])

    def rsum_copy(k):
        t, device = zpeer(k)
        return copy(RSUM, k, rss.at[t], rsr.at[k], device)

    def lsum_copy(k):
        t, device = qpeer(k)
        return copy(LSUM, k, lss.at[t], lsr.at[k], device)

    def w1_copy(k):
        t, device = dpeer(k)
        return copy(W1, k, wgs.at[t], wgr.at[k], device)

    def w2_copy(k):
        t, device = zpeer(k)
        return copy(W2, k, w2s.at[t], w2r.at[k], device)

    def w3_copy(k):
        return copy(W3, k, w3.at[q], w3.at[q], qpeer(k)[1])

    def w4_copy(k):
        block = w5.at[depth, pl.ds(pl.multiple_of(z * 16, 16), 16)]
        return copy(W4, k, block, block, zpeer(k)[1])

    def w5_copy(k):
        return copy(W5, k, w5.at[depth], w5.at[depth], dpeer(k)[1])

    def s1_copy(k):
        t, device = zpeer(k)
        return copy(S1, k, sm.at[t], s1.at[z], device)

    def s2_copy(k):
        return copy(S2, k, s2.at[q], s2.at[q], qpeer(k)[1])

    def s3_copy(k):
        return copy(S3, k, s3.at[depth], s3.at[depth], dpeer(k)[1])

    def s4_copy(k):
        return copy(S4, k, sf.at[z], sf.at[z], zpeer(k)[1])

    def start(make, count=8):
        for k in range(1, count):
            make(k).start()

    def arrived(make, count=8):
        for k in range(1, count):
            make(k).wait_recv()

    barrier = pltpu.get_barrier_semaphore()
    for k in range(1, 8):
        pl.semaphore_signal(barrier, inc=1, device_id=zpeer(k)[1], device_id_type=MESH)
        pl.semaphore_signal(barrier, inc=1, device_id=qpeer(k)[1], device_id_type=MESH)
    for k in range(1, 4):
        pl.semaphore_signal(barrier, inc=1, device_id=dpeer(k)[1], device_id_type=MESH)

    used = jnp.sum(seq_ref[...].astype(F32), axis=1, keepdims=True)
    res_j = res_ref[:, pl.ds(pl.multiple_of(col * 128, 128), 128)].astype(F32)
    res_j = jnp.broadcast_to(res_j, (128, 128)).T
    inv1[...] = 1.0 / jnp.maximum(used * res_j, 1.0)

    @pl.loop(0, 32)
    def _(i):
        res_i = res_s[row * 32 + i].astype(F32)
        scaled = pair_ref[i].astype(F32) * (inv1[...] * res_i + (1.0 - res_i))
        for t in range(8):
            piece = jnp.concatenate([scaled[t * 8 : t * 8 + 8], scaled[64 + t * 8 : 72 + t * 8]], axis=0)
            ps[t, i] = piece.astype(BF16)

    pl.semaphore_wait(barrier, 17)
    start(pair_copy)
    own_pair = pltpu.make_async_copy(ps.at[q], scb.at[col, pl.ds(h * 32, 32)], local_sem)
    own_pair.start()

    pick = lax.broadcasted_iota(jnp.int32, (64, 32), 0) - lax.broadcasted_iota(jnp.int32, (64, 32), 1)
    first, second = (pick == 0).astype(F32), (pick == 32).astype(F32)
    wt[...] = (dot_nt(first.astype(BF16), wl_ref[...]) + dot_nt(second.astype(BF16), wr_ref[...])).astype(BF16)
    exact = dict(precision=lax.Precision.HIGHEST)
    bias[...] = dot_nt(first, jnp.broadcast_to(lb_ref[...], (128, 32)), **exact) + dot_nt(
        second, jnp.broadcast_to(rb_ref[...], (128, 32)), **exact
    )
    for e in range(2):
        xf[e] = x_ref[:, e * 128 : e * 128 + 128].astype(F32)
    seq_row = seq_ref[:, pl.ds(pl.multiple_of(depth * 128, 128), 128)].astype(F32)
    own_first = (row * 4 + col) * 8

    @pl.loop(0, 8)
    def _(r):
        values = jnp.concatenate([xf[e, pl.ds(r, 128, stride=8), :] for e in range(2)], axis=1)
        centred = values - jnp.mean(values, axis=1, keepdims=True)
        inv_std = lax.rsqrt(jnp.mean(centred * centred, axis=1, keepdims=True) + 1e-05)
        units = centred * inv_std
        normed = (units * gain_ref[...] + shift_ref[...]).astype(BF16)
        unit[r] = units
        norm[r] = normed
        istd[r] = jnp.broadcast_to(inv_std, (128, 128))
        mask = seq_row * res_s[own_first + r].astype(F32)
        both = (dot_nt(wt[...], normed) + bias[...]) * mask
        lb[pl.ds(pl.multiple_of(q * 256 + r * 32, 32), 32), :] = both[:32].astype(BF16)
        rf[pl.ds(r, 32, stride=8), :] = both[32:]

    rbuf[z] = rf[...].astype(BF16)
    start(left_copy)
    start(right_copy)

    wf[...] = ow_ref[...].astype(F32)
    for d in range(32):
        wp[d // 2 * 32 : d // 2 * 32 + 32, d % 2 * 128 : d % 2 * 128 + 128] = wf[pl.ds(d, 32, stride=32), :].astype(BF16)

    @pl.loop(0, 64)
    def _(i):
        bd[i] = jnp.zeros((128, 256), BF16)

    own_pair.wait()
    arrived(pair_copy)

    @pl.loop(0, 32)
    def _(t):
        for e in range(2):
            block = jnp.concatenate([scb[y, 2 * t + e] for y in range(4)], axis=0)
            bd[2 * t + e, :64, :128] = block
            bd[2 * t + e, 64:, 128:] = block
        grads = dot_nt(wp[...], bd[pl.ds(2 * t, 2)].reshape(256, 256)).astype(BF16)
        for e in range(2):
            at = pl.ds(pl.multiple_of((2 * t + e) * 32, 32), 32)
            for p in range(16):
                og[at, p * 128 : p * 128 + 128] = grads[p * 32 : p * 32 + 32, e * 128 : e * 128 + 128]

    arrived(left_copy)
    for t in range(16):
        block = lb[t * 128 : t * 128 + 128, :].astype(F32)
        lt[:, t * 128 : t * 128 + 128] = block.T.astype(BF16)

    @pl.loop(0, 8)
    def _(n):
        sums = dot(lt[...], og[:, pl.ds(pl.multiple_of(n * 256, 256), 256)])
        for e in range(2):
            turned = sums[:, e * 128 : e * 128 + 128].T
            for t in range(8):
                piece = jnp.concatenate([turned[t * 8 : t * 8 + 8], turned[64 + t * 8 : 72 + t * 8]], axis=0)
                rss[t, pl.ds(pl.multiple_of((2 * n + e) * 16, 16), 16), :] = piece.astype(BF16)

    start(rsum_copy)

    arrived(right_copy)

    @pl.loop(0, 16)
    def _(p):
        blocks = [rbuf[t, pl.ds(pl.multiple_of(p * 16, 16), 16), :].astype(F32) for t in range(8)]
        rows = [block[:8] for block in blocks] + [block[8:] for block in blocks]
        rt[pl.ds(pl.multiple_of(p * 128, 128), 128), :] = jnp.concatenate(rows, axis=0).astype(BF16)

    def left_sum(t):
        at = pl.ds(pl.multiple_of(t * 256, 256), 256)
        lss[t] = dot(og[at, :], rt[...]).astype(BF16)

    @pl.loop(1, 8)
    def _(k):
        left_sum(lax.rem(q + k, 8))
        lsum_copy(k).start()

    left_sum(q)

    @pl.loop(0, 8)
    def _(n):
        at = pl.ds(pl.multiple_of(n * 256, 256), 256)
        for m in range(4):
            product = dot_nt(lb[m * 512 : m * 512 + 512, :], rt[at, :])
            outer[m * 512 : m * 512 + 512, at] = product.astype(BF16)

    wga[...] = jnp.zeros_like(wga)

    @pl.loop(0, 16)
    def _(t):
        blocks = [outer[pl.ds(pl.multiple_of((4 * t + e) * 32, 32), 32), :] for e in range(4)]
        rows = [
            jnp.concatenate([block[:, p * 128 : p * 128 + 128] for block in blocks], axis=1) for p in range(16)
        ]
        wga[...] += dot(jnp.concatenate(rows, axis=0), bd[pl.ds(4 * t, 4)].reshape(512, 256))

    for t in range(4):
        wgs[t] = wga[t * 128 : t * 128 + 128, :].astype(BF16)
    start(w1_copy, 4)

    arrived(lsum_copy)
    total = lss[q].astype(F32)
    for k in range(1, 8):
        total = total + lsr[k].astype(F32)
    lsf[...] = total
    arrived(rsum_copy)
    total = rss[z].astype(F32)
    for k in range(1, 8):
        total = total + rsr[k].astype(F32)
    rf[...] = total

    wgt[...] = jnp.zeros_like(wgt)
    extra[...] = jnp.zeros_like(extra)

    @pl.loop(0, 8)
    def _(r):
        mask = seq_row * res_s[own_first + r].astype(F32)
        sides = [lsf[pl.ds(pl.multiple_of(r * 32, 32), 32), :], rf[pl.ds(r, 32, stride=8), :]]
        pre = (jnp.concatenate(sides, axis=0) * mask).astype(BF16)
        grad = lax.dot_general(pre, wt[...], TN, preferred_element_type=F32)
        ngrad[r] = grad
        wgt[...] += dot(pre, norm[r])
        extra[0:1, :] += jnp.sum(grad * unit[r], axis=0, keepdims=True)
        extra[1:2, :] += jnp.sum(grad, axis=0, keepdims=True)
        extra[2:3, 0:64] += dot_nt(jnp.ones((8, 128), BF16), pre)[0:1]

    for t in range(8):
        sm[t, 0:8] = wgt[t * 8 : t * 8 + 8, :]
        sm[t, 8:16] = extra[...]
    s1[z] = sm[z]
    start(s1_copy)

    def input_grad(r):
        units = unit[r]
        weighted = ngrad[r] * gain_ref[...]
        mean = jnp.mean(weighted, axis=1, keepdims=True)
        along = jnp.mean(weighted * units, axis=1, keepdims=True)
        scale = jnp.concatenate([istd[r], istd[r]], axis=1)
        result = scale * (weighted - mean - units * along)
        for e in range(2):
            xf[e, pl.ds(r, 128, stride=8), :] = result[:, e * 128 : e * 128 + 128]

    def summed(ref, count):
        total = ref[0]
        for k in range(1, count):
            total = total + ref[k]
        return total

    arrived(w1_copy, 4)
    total = wga[pl.ds(pl.multiple_of(depth * 128, 128), 128), :]
    for k in range(1, 4):
        total = total + wgr[k].astype(F32)
    w1f[...] = total
    for t in range(8):
        w2s[t] = w1f[t * 16 : t * 16 + 16, :].astype(BF16)
    start(w2_copy)

    @pl.loop(0, 3)
    def _(r):
        input_grad(r)

    arrived(s1_copy)
    s2[q] = summed(s1, 8)
    start(s2_copy)

    arrived(w2_copy)
    total = w1f[pl.ds(pl.multiple_of(z * 16, 16), 16), :]
    for k in range(1, 8):
        total = total + w2r[k].astype(F32)
    w3[q] = total
    start(w3_copy)

    @pl.loop(3, 6)
    def _(r):
        input_grad(r)

    arrived(s2_copy)
    s3[depth] = summed(s2, 8)
    start(s3_copy, 4)

    arrived(w3_copy)
    w5[depth, pl.ds(pl.multiple_of(z * 16, 16), 16), :] = summed(w3, 8).astype(BF16)
    start(w4_copy)

    @pl.loop(6, 8)
    def _(r):
        input_grad(r)

    arrived(s3_copy, 4)
    total = summed(s3, 4)
    sf[z] = total[:8]
    start(s4_copy)
    small_ref[64:72, :] = total[8:]

    arrived(w4_copy)
    start(w5_copy, 4)

    for e in range(2):
        ag_ref[:, e * 128 : e * 128 + 128] = xf[e].astype(BF16)

    arrived(s4_copy)
    for t in range(8):
        small_ref[t * 8 : t * 8 + 8, :] = sf[t]
    arrived(w5_copy, 4)
    for t in range(4):
        wg_ref[t * 128 : t * 128 + 128, :] = w5[t]

    for make in (pair_copy, left_copy, right_copy, rsum_copy, lsum_copy, w2_copy, w3_copy, w4_copy, s1_copy, s2_copy,
                 s4_copy):
        for k in range(1, 8):
            make(k).wait_send()
    for make in (w1_copy, w5_copy, s3_copy):
        for k in range(1, 4):
            make(k).wait_send()


def last_kernel(ag_in, small, wg, ag_ref, lw_ref, lb_ref, rw_ref, rb_ref, gain_ref, shift_ref, ow_ref):
    ag_ref[...] = ag_in[...]
    turned = small[0:64, :].T
    lw_ref[...] = turned[:, :32]
    rw_ref[...] = turned[:, 32:]
    gain_ref[...] = small[64:65, :]
    shift_ref[...] = small[65:66, :]
    lb_ref[...] = small[66:67, 0:32]
    rb_ref[...] = small[66:67, 32:64]
    for d in range(32):
        tile = wg[d // 2 * 32 : d // 2 * 32 + 32, d % 2 * 128 : d % 2 * 128 + 128]
        ow_ref[pl.ds(d, 32, stride=32), :] = tile.astype(F32)


def body(
    alignment, seq_mask, residue_mask, layer_norm_gain, layer_norm_bias, left_projection_weight, left_bias,
    right_projection_weight, right_bias, out_weight, pair_grad,
):
    vmem = pl.BlockSpec(memory_space=pltpu.VMEM)
    smem = pl.BlockSpec(memory_space=pltpu.SMEM)
    v = pltpu.VMEM
    shape = jax.ShapeDtypeStruct
    scratch = [
        v((128, 128), F32),
        v((2, 1024, 128), F32),
        v((8, 128, 256), F32),
        v((8, 128, 256), BF16),
        v((8, 128, 128), F32),
        v((8, 128, 256), F32),
        v((64, 256), BF16),
        v((64, 128), F32),
        v((1024, 128), F32),
        v((512, 256), BF16),
        v((8, 32, 16, 128), BF16),
        v((4, 64, 16, 128), BF16),
        v((64, 128, 256), BF16),
        v((2048, 2048), BF16),
        v((2048, 2048), BF16),
        v((2048, 128), BF16),
        v((128, 2048), BF16),
        v((256, 128), F32),
        v((8, 256, 128), BF16),
        v((2048, 128), BF16),
        v((8, 256, 128), BF16),
        v((8, 256, 128), BF16),
        v((8, 256, 128), BF16),
        v((8, 256, 128), BF16),
        v((256, 128), F32),
        v((512, 256), F32),
        v((4, 128, 256), BF16),
        v((4, 128, 256), BF16),
        v((128, 256), F32),
        v((8, 16, 256), BF16),
        v((8, 16, 256), BF16),
        v((8, 16, 256), F32),
        v((4, 128, 256), BF16),
        v((64, 256), F32),
        v((8, 256), F32),
        v((8, 16, 256), F32),
        v((8, 16, 256), F32),
        v((8, 16, 256), F32),
        v((4, 16, 256), F32),
        v((8, 8, 256), F32),
        pltpu.SemaphoreType.DMA((14, 8)),
        pltpu.SemaphoreType.DMA((14, 8)),
        pltpu.SemaphoreType.DMA,
    ]
    ag, small, wg = pl.pallas_call(
        main_kernel,
        out_shape=(shape((1024, 256), BF16), shape((72, 256), F32), shape((512, 256), BF16)),
        in_specs=[vmem] * 3 + [smem] + [vmem] * 8,
        out_specs=(vmem,) * 3,
        scratch_shapes=scratch,
        compiler_params=pltpu.CompilerParams(
            collective_id=0, has_side_effects=True, vmem_limit_bytes=58 * 1024 * 1024
        ),
        name="pair_backward",
    )(
        alignment.reshape(1024, 256), seq_mask.reshape(1, 512), residue_mask.reshape(1, 512), residue_mask,
        layer_norm_gain.reshape(1, 256), layer_norm_bias.reshape(1, 256), left_projection_weight,
        left_bias.reshape(1, 32), right_projection_weight, right_bias.reshape(1, 32), out_weight, pair_grad,
    )
    ag, lw, lbg, rw, rbg, gain, shift, ow = pl.pallas_call(
        last_kernel,
        out_shape=(
            shape((1024, 256), BF16), shape((256, 32), F32), shape((1, 32), F32), shape((256, 32), F32),
            shape((1, 32), F32), shape((1, 256), F32), shape((1, 256), F32), shape((1024, 128), F32),
        ),
        in_specs=[vmem] * 3,
        out_specs=(vmem,) * 8,
        compiler_params=pltpu.CompilerParams(vmem_limit_bytes=32 * 1024 * 1024),
        name="lay_out",
    )(ag, small, wg)
    return (
        ag.reshape(128, 8, 256), lw, lbg.reshape(32), rw, rbg.reshape(32), gain.reshape(256), shift.reshape(256), ow,
    )


def solution(mesh):
    placed = (P("depth", ("row", "col"), None),) + (P(),) * 9 + (P("row", "col", None),)
    return jax.shard_map(
        body,
        mesh=mesh,
        in_specs=placed,
        out_specs=(P("depth", ("row", "col"), None),) + (P(),) * 7,
        check_vma=False,
    )
```

time: 943 us -> 88.2 us (0.09)
  waiting for transfers between devices: 820 us -> 0 us
  Pallas kernels: 0 us -> 80.8 us
  local copies, waits for them, and re-layouts: 51.9 us -> 6.44 us
  matrix products: 34.6 us -> 0 us
  between operations: 14.3 us -> 0.66 us
  blocking collectives: 11.2 us -> 0 us
    psum x3 -> x0, waiting for transfers between devices: 653 us -> none  [the longest x2 504 us: body(): lax.psum((out_weight_part, left_weight_part, left_bias_part, right_weight...]
    all_gather x1 -> x0, waiting for transfers between devices: 113 us -> none  [body(): right_every = lax.all_gather(right_own, ('row', 'col'), axis=0, tiled=True)]
    pallas_call x0 -> x2, Pallas kernels: none -> 80.8 us  [the longest x1 79.5 us: body(): pl.pallas_call(main_kernel, out_shape=(shape((1024, 256), BF16), shape((7...]
    reduce_scatter x2 -> x0, waiting for transfers between devices: 51.8 us -> none  [the longest x1 29.6 us: body(): lax.psum_scatter(left_rows_grad.astype(jnp.bfloat16), 'col', scatter_dime...]
    dot_general x26 -> x0, matrix products: 34.6 us -> none  [the longest x4 9.33 us: one_block(): jnp.dot(outer_flat.T, scaled_flat, preferred_element_type=jnp.float32)]
    while x61 -> x0, local copies, waits for them, and re-layouts: 19.2 us -> none
    convert_element_type x9 -> x0, local copies, waits for them, and re-layouts: 16.5 us -> none  [the longest x4 10.3 us: one_block(): jnp.dot(scaled_flat, out_weight.T, preferred_element_type=jnp.float32)]
    all_gather x1 -> x0, blocking collectives: 11.2 us -> none  [body(): left_rows = lax.all_gather(left_own, 'col', axis=0, tiled=True)]
  transfers between devices with their start and end apart: 6 -> 0, of which waited for: 6 -> 0; matrix products, arithmetic and copies ran while one was open for 2% -> 0% of each run, Pallas kernels for 0% -> 0%
where the time goes in v1:
time: 88.2 us; the launch traced here: 87.9 us
  Pallas kernels  80.8 us (92%)
  local copies, waits for them, and re-layouts  6.44 us (7%)
    pallas_call x1, Pallas kernels, body(): pl.pallas_call(main_kernel, out_shape=(shape((1024, 256), BF16), shape((7...  79.5 us
    unnamed x12, local copies, waits for them, and re-layouts  6.44 us

profile of v1, /device:TPU:1, one launch (start us, length us, event | category | flops | bytes accessed | tf_op | source)
XLA Modules:
  0.0 87.9 jit_solution(16238021641213381930)
XLA Ops:
  0.6 0.0 copy-start.3
  0.6 1.5 %copy.19.wl_ref = bf16[256,32]{1,0:T(8,128)(2,1)} copy(bf16[256,32]{0,1:T(8,128)(2,1)} %param.16) | data formatting | bytes 32768 | tf_op args[5]
  2.1 0.0 copy-done.3
  2.1 0.7 copy.20.wr_ref
  2.8 79.5 %pair_backward.1 = (bf16[1024,256]{1,0:T(8,128)(2,1)}, f32[72,256]{1,0:T(8,128)}, bf16[512,256]{1,0:T(8,128)(2,1)}) custom-call(bf16[1024,256]{1,0:T(8,128)(2,1)} %bitcast.12, s32[1,512]{1,0:T(1,128)} %bitcast.14, s32[1,512]{1,0:T(1,128)} %bitcast.13, s32[512]{0:T(512)} %res_s.1, f32[1,256]{1,0:T(1,128)} %bitcast.15, f32[1,256]{1,0:T(1,128)} %bitcast.16, ...), custom_call_target="tpu_custom_call" | custom-call | tf_op jit(solution)/shard_map/pair_backward/pallas_call | solution.py:428
  82.3 0.0 copy-start
  82.3 1.0 %copy-done = bf16[1024,256]{1,0:T(8,128)(2,1)S(1)} copy-done((bf16[1024,256]{1,0:T(8,128)(2,1)S(1)}, bf16[1024,256]{1,0:T(8,128)(2,1)}, u32[]{:S(2)}) %copy-start) | copy-done | bytes 524312
  83.4 0.0 copy-start.1
  83.4 0.9 %copy-done.1 = bf16[512,256]{1,0:T(8,128)(2,1)S(1)} copy-done((bf16[512,256]{1,0:T(8,128)(2,1)S(1)}, bf16[512,256]{1,0:T(8,128)(2,1)}, u32[]{:S(2)}) %copy-start.1) | copy-done | bytes 262168
  84.3 0.0 copy-start.2
  84.3 0.9 %copy-done.2 = f32[72,256]{1,0:T(8,128)S(1)} copy-done((f32[72,256]{1,0:T(8,128)S(1)}, f32[72,256]{1,0:T(8,128)}, u32[]{:S(2)}) %copy-start.2) | copy-done | bytes 73752
  85.2 1.3 %lay_out.1 = (bf16[1024,256]{1,0:T(8,128)(2,1)}, f32[256,32]{1,0:T(8,128)S(1)}, f32[1,32]{1,0:T(1,128)}, f32[256,32]{1,0:T(8,128)S(1)}, f32[1,32]{1,0:T(1,128)},...) custom-call(bf16[1024,256]{1,0:T(8,128)(2,1)S(1)} %copy-done, f32[72,256]{1,0:T(8,128)S(1)} %copy-done.2, ...), custom_call_target="tpu_custom_call" | custom-call | tf_op jit(solution)/shard_map/lay_out/pallas_call | solution.py:443
  86.5 0.7 copy.21
  87.2 0.7 copy.22
Async XLA Ops:
  0.6 1.5 %copy-start.3 = (bf16[256,32]{0,1:T(8,128)(2,1)S(1)}, bf16[256,32]{0,1:T(8,128)(2,1)}, u32[]{:S(2)}) copy-start(bf16[256,32]{0,1:T(8,128)(2,1)} %param.18) | copy-start | bytes 49156
  82.3 1.0 %copy-start = (bf16[1024,256]{1,0:T(8,128)(2,1)S(1)}, bf16[1024,256]{1,0:T(8,128)(2,1)}, u32[]{:S(2)}) copy-start(bf16[1024,256]{1,0:T(8,128)(2,1)} %get-tuple-element.19.ag_in) | copy-start | bytes 1572868
  83.4 0.9 %copy-start.1 = (bf16[512,256]{1,0:T(8,128)(2,1)S(1)}, bf16[512,256]{1,0:T(8,128)(2,1)}, u32[]{:S(2)}) copy-start(bf16[512,256]{1,0:T(8,128)(2,1)} %get-tuple-element.21.wg) | copy-start | bytes 786436
  84.3 0.9 %copy-start.2 = (f32[72,256]{1,0:T(8,128)S(1)}, f32[72,256]{1,0:T(8,128)}, u32[]{:S(2)}) copy-start(f32[72,256]{1,0:T(8,128)} %get-tuple-element.20.small) | copy-start | bytes 221188

commit v2 on v1

v2 whole, which is shorter than its diff:
```python
import jax
import jax.numpy as jnp
from jax import lax
from jax.experimental import pallas as pl
from jax.experimental.pallas import tpu as pltpu
from jax.sharding import PartitionSpec as P

F32, BF16 = jnp.float32, jnp.bfloat16
MESH = pl.DeviceIdType.MESH
NT = (((1,), (1,)), ((), ()))
TN = (((0,), (0,)), ((), ()))
PAIR, LEFT, RIGHT, RSUM, RSUM2, LSUM = range(6)
W1, W2, W3, S1, S2, S3 = range(6)


def dot(a, b):
    return jnp.dot(a, b, preferred_element_type=F32)


def dot_nt(a, b, **kw):
    return lax.dot_general(a, b, NT, preferred_element_type=F32, **kw)


def main_kernel(
    x_ref, seq_ref, res_ref, res_s, gain_ref, shift_ref, wl_ref, lb_ref, wr_ref, rb_ref, ow_ref, pair_ref,
    ag_ref, sf_ref, wg_ref,
    inv1, xf, unit, norm, istd, ngrad, wt, bias, wf, wp, ps, scb, bd, og, outer, lb, lt, rf, rbuf, rt,
    rss, rsr, lss, lsr, lsf, wga, w1s, w1r, w2, w3, wgt, extra, s1s, s1r, s2, s3,
    send_sem, recv_sem, group_send, group_recv, local_sem,
):
    depth, row, col = lax.axis_index("depth"), lax.axis_index("row"), lax.axis_index("col")
    z, h = lax.div(row, 2), lax.rem(row, 2)
    q = h * 4 + col

    def zpeer(k):
        t = lax.rem(z + k, 8)
        return t, (depth, t * 2 + h, col)

    def qpeer(k):
        t = lax.rem(q + k, 8)
        return t, (depth, z * 2 + lax.div(t, 4), lax.rem(t, 4))

    g = depth * 8 + q

    def gpeer(k):
        t = lax.rem(g + k, 32)
        u = lax.rem(t, 8)
        return t, (lax.div(t, 8), z * 2 + lax.div(u, 4), lax.rem(u, 4))

    def copy(which, k, src, dst, device):
        return pltpu.make_async_remote_copy(
            src_ref=src, dst_ref=dst, send_sem=send_sem.at[which, k], recv_sem=recv_sem.at[which, k],
            device_id=device, device_id_type=MESH,
        )

    def pair_copy(k):
        t, device = qpeer(k)
        return copy(PAIR, k, ps.at[t], scb.at[col, pl.ds(h * 32, 32)], device)

    def left_copy(k):
        block = lb.at[pl.ds(pl.multiple_of(q * 256, 256), 256)]
        return copy(LEFT, k, block, block, qpeer(k)[1])

    def right_copy(k):
        return copy(RIGHT, k, rbuf.at[z], rbuf.at[z], zpeer(k)[1])

    def rsum_copy(k, part=0):
        t, device = zpeer(k)
        half = pl.ds(part * 128, 128)
        return copy(RSUM + part, k, rss.at[t, half], rsr.at[k, half], device)

    def rsum2_copy(k):
        return rsum_copy(k, 1)

    def lsum_copy(k):
        t, device = qpeer(k)
        return copy(LSUM, k, lss.at[t], lsr.at[k], device)

    def group_copy(which, src, dst, device):
        return pltpu.make_async_remote_copy(
            src_ref=src, dst_ref=dst, send_sem=group_send.at[which], recv_sem=group_recv.at[which],
            device_id=device, device_id_type=MESH,
        )

    def scatter_plane(which, src, dst):
        @pl.loop(1, 32)
        def _(k):
            t, device = gpeer(k)
            group_copy(which, src.at[t], dst.at[k], device).start()

    def share_line(which, ref):
        for k in range(1, 8):
            group_copy(which, ref.at[z], ref.at[z], zpeer(k)[1]).start()

    def gather_plane(which, ref):
        @pl.loop(1, 32)
        def _(k):
            group_copy(which, ref.at[g], ref.at[g], gpeer(k)[1]).start()

    def group_wait(which, ref, sems):
        count = ref.shape[0] - 1
        pltpu.make_async_copy(ref.at[pl.ds(1, count)], ref.at[pl.ds(1, count)], sems.at[which]).wait()

    def start(make, count=8):
        for k in range(1, count):
            make(k).start()

    def arrived(make, count=8):
        for k in range(1, count):
            make(k).wait_recv()

    barrier = pltpu.get_barrier_semaphore()
    for k in range(1, 8):
        pl.semaphore_signal(barrier, inc=1, device_id=zpeer(k)[1], device_id_type=MESH)

    @pl.loop(1, 32)
    def _(k):
        pl.semaphore_signal(barrier, inc=1, device_id=gpeer(k)[1], device_id_type=MESH)

    used = jnp.sum(seq_ref[...].astype(F32), axis=1, keepdims=True)
    res_j = res_ref[:, pl.ds(pl.multiple_of(col * 128, 128), 128)].astype(F32)
    res_j = jnp.broadcast_to(res_j, (128, 128)).T
    inv1[...] = 1.0 / jnp.maximum(used * res_j, 1.0)

    @pl.loop(0, 32)
    def _(i):
        res_i = res_s[row * 32 + i].astype(F32)
        scaled = pair_ref[i].astype(F32) * (inv1[...] * res_i + (1.0 - res_i))
        for t in range(8):
            piece = jnp.concatenate([scaled[t * 8 : t * 8 + 8], scaled[64 + t * 8 : 72 + t * 8]], axis=0)
            ps[t, i] = piece.astype(BF16)

    pl.semaphore_wait(barrier, 38)
    start(pair_copy)
    own_pair = pltpu.make_async_copy(ps.at[q], scb.at[col, pl.ds(h * 32, 32)], local_sem)
    own_pair.start()

    pick = lax.broadcasted_iota(jnp.int32, (64, 32), 0) - lax.broadcasted_iota(jnp.int32, (64, 32), 1)
    first, second = (pick == 0).astype(F32), (pick == 32).astype(F32)
    wt[0:32, :] = wl_ref[...]
    wt[32:64, :] = wr_ref[...]
    exact = dict(precision=lax.Precision.HIGHEST)
    bias[...] = dot_nt(first, jnp.broadcast_to(lb_ref[...], (128, 32)), **exact) + dot_nt(
        second, jnp.broadcast_to(rb_ref[...], (128, 32)), **exact
    )
    for e in range(2):
        xf[e] = x_ref[:, e * 128 : e * 128 + 128].astype(F32)
    seq_row = seq_ref[:, pl.ds(pl.multiple_of(depth * 128, 128), 128)].astype(F32)
    own_first = (row * 4 + col) * 8

    @pl.loop(0, 8, unroll=4)
    def _(r):
        values = jnp.concatenate([xf[e, pl.ds(r, 128, stride=8), :] for e in range(2)], axis=1)
        centred = values - jnp.mean(values, axis=1, keepdims=True)
        inv_std = lax.rsqrt(jnp.mean(centred * centred, axis=1, keepdims=True) + 1e-05)
        units = centred * inv_std
        normed = (units * gain_ref[...] + shift_ref[...]).astype(BF16)
        unit[r] = units
        norm[r] = normed
        istd[r] = jnp.broadcast_to(inv_std, (128, 128))
        mask = seq_row * res_s[own_first + r].astype(F32)
        both = (dot_nt(wt[...], normed) + bias[...]) * mask
        lb[pl.ds(pl.multiple_of(q * 256 + r * 32, 32), 32), :] = both[:32].astype(BF16)
        rf[pl.ds(r, 32, stride=8), :] = both[32:]

    rbuf[z] = rf[...].astype(BF16)
    start(left_copy)
    start(right_copy)

    wf[...] = ow_ref[...].astype(F32)
    for d in range(32):
        wp[d // 2 * 32 : d // 2 * 32 + 32, d % 2 * 128 : d % 2 * 128 + 128] = wf[pl.ds(d, 32, stride=32), :].astype(BF16)

    @pl.loop(0, 64)
    def _(i):
        bd[i] = jnp.zeros((128, 256), BF16)

    own_pair.wait()
    arrived(pair_copy)

    @pl.loop(0, 32, unroll=8)
    def _(t):
        for e in range(2):
            block = jnp.concatenate([scb[y, 2 * t + e] for y in range(4)], axis=0)
            bd[2 * t + e, :64, :128] = block
            bd[2 * t + e, 64:, 128:] = block
        grads = dot_nt(wp[...], bd[pl.ds(2 * t, 2)].reshape(256, 256)).astype(BF16)
        for e in range(2):
            at = pl.ds(pl.multiple_of((2 * t + e) * 32, 32), 32)
            for p in range(16):
                og[at, p * 128 : p * 128 + 128] = grads[p * 32 : p * 32 + 32, e * 128 : e * 128 + 128]

    arrived(left_copy)
    for t in range(16):
        block = lb[t * 128 : t * 128 + 128, :].astype(F32)
        lt[:, t * 128 : t * 128 + 128] = block.T.astype(BF16)

    def right_sums(part):
        sums = dot(lt[...], og[:, part * 1024 : part * 1024 + 1024])
        for p in range(8):
            turned = sums[:, p * 128 : p * 128 + 128].T
            at = part * 128 + p * 16
            for t in range(8):
                piece = jnp.concatenate([turned[t * 8 : t * 8 + 8], turned[64 + t * 8 : 72 + t * 8]], axis=0)
                rss[t, at : at + 16, :] = piece.astype(BF16)

    right_sums(0)
    start(rsum_copy)
    right_sums(1)
    start(rsum2_copy)

    arrived(right_copy)

    @pl.loop(0, 16)
    def _(p):
        blocks = [rbuf[t, pl.ds(pl.multiple_of(p * 16, 16), 16), :].astype(F32) for t in range(8)]
        rows = [block[:8] for block in blocks] + [block[8:] for block in blocks]
        rt[pl.ds(pl.multiple_of(p * 128, 128), 128), :] = jnp.concatenate(rows, axis=0).astype(BF16)

    def left_sum(t):
        at = pl.ds(pl.multiple_of(t * 256, 256), 256)
        lss[t] = dot(og[at, :], rt[...]).astype(BF16)

    @pl.loop(1, 8)
    def _(k):
        left_sum(lax.rem(q + k, 8))
        lsum_copy(k).start()

    left_sum(q)

    @pl.loop(0, 8, unroll=4)
    def _(n):
        at = pl.ds(pl.multiple_of(n * 256, 256), 256)
        for m in range(4):
            product = dot_nt(lb[m * 512 : m * 512 + 512, :], rt[at, :])
            outer[m * 512 : m * 512 + 512, at] = product.astype(BF16)

    wga[...] = jnp.zeros_like(wga)

    @pl.loop(0, 4)
    def _(t):
        blocks = [outer[pl.ds(pl.multiple_of((16 * t + e) * 32, 32), 32), :] for e in range(16)]
        rows = [
            jnp.concatenate([block[:, p * 128 : p * 128 + 128] for block in blocks], axis=1) for p in range(16)
        ]
        wga[...] += dot(jnp.concatenate(rows, axis=0), bd[pl.ds(16 * t, 16)].reshape(2048, 256))

    for t in range(32):
        w1s[t] = wga[t * 16 : t * 16 + 16, :].astype(BF16)
    scatter_plane(W1, w1s, w1r)

    arrived(lsum_copy)
    total = lss[q].astype(F32)
    for k in range(1, 8):
        total = total + lsr[k].astype(F32)
    lsf[...] = total
    arrived(rsum_copy)
    arrived(rsum2_copy)
    total = rss[z].astype(F32)
    for k in range(1, 8):
        total = total + rsr[k].astype(F32)
    rf[...] = total

    wgt[...] = jnp.zeros_like(wgt)
    extra[...] = jnp.zeros_like(extra)

    @pl.loop(0, 8, unroll=4)
    def _(r):
        mask = seq_row * res_s[own_first + r].astype(F32)
        sides = [lsf[pl.ds(pl.multiple_of(r * 32, 32), 32), :], rf[pl.ds(r, 32, stride=8), :]]
        pre = (jnp.concatenate(sides, axis=0) * mask).astype(BF16)
        grad = lax.dot_general(pre, wt[...], TN, preferred_element_type=F32)
        ngrad[r] = grad
        wgt[...] += dot(pre, norm[r])
        extra[0:1, :] += jnp.sum(grad * unit[r], axis=0, keepdims=True)
        extra[1:2, :] += jnp.sum(grad, axis=0, keepdims=True)
        extra[2:3, 0:64] += dot_nt(jnp.ones((8, 128), BF16), pre)[0:1]

    upper = lax.broadcasted_iota(jnp.int32, (8, 128), 0) < 4
    for t in range(16):
        tile = wgt[t // 2 * 8 : t // 2 * 8 + 8, t % 2 * 128 : t % 2 * 128 + 128]
        s1s[2 * t] = jnp.where(upper, tile, 0.0)
        s1s[2 * t + 1] = jnp.where(upper, 0.0, tile)
    s1s[0, 4:5, :] = extra[0:1, :128]
    s1s[1, 0:1, :] = extra[0:1, 128:]
    s1s[2, 4:5, :] = extra[1:2, :128]
    s1s[3, 0:1, :] = extra[1:2, 128:]
    s1s[4, 4:5, :] = extra[2:3, :128]
    scatter_plane(S1, s1s, s1r)

    def input_grad(r):
        units = unit[r]
        weighted = ngrad[r] * gain_ref[...]
        mean = jnp.mean(weighted, axis=1, keepdims=True)
        along = jnp.mean(weighted * units, axis=1, keepdims=True)
        scale = jnp.concatenate([istd[r], istd[r]], axis=1)
        result = scale * (weighted - mean - units * along)
        for e in range(2):
            xf[e, pl.ds(r, 128, stride=8), :] = result[:, e * 128 : e * 128 + 128]

    def summed(ref, count, first):
        total = first
        for k in range(1, count):
            total = total + ref[k].astype(F32)
        return total

    @pl.loop(0, 4, unroll=4)
    def _(r):
        input_grad(r)

    group_wait(W1, w1r, group_recv)
    w2[z] = summed(w1r, 32, wga[pl.ds(pl.multiple_of(g * 16, 16), 16), :]).astype(BF16)
    share_line(W2, w2)
    group_wait(S1, s1r, group_recv)
    s2[z] = summed(s1r, 32, s1s[g])
    share_line(S2, s2)

    @pl.loop(4, 8, unroll=4)
    def _(r):
        input_grad(r)

    for e in range(2):
        ag_ref[:, e * 128 : e * 128 + 128] = xf[e].astype(BF16)

    group_wait(W2, w2, group_recv)
    w3[g] = summed(w2, 8, w2[0].astype(F32)).astype(BF16)
    gather_plane(W3, w3)
    group_wait(S2, s2, group_recv)
    s3[g] = summed(s2, 8, s2[0])
    gather_plane(S3, s3)

    for make in (pair_copy, left_copy, right_copy, rsum_copy, rsum2_copy, lsum_copy):
        for k in range(1, 8):
            make(k).wait_send()
    for which, ref in ((W1, w1s), (W2, w2), (W3, w3), (S1, s1s), (S2, s2), (S3, s3)):
        group_wait(which, ref, group_send)

    group_wait(W3, w3, group_recv)
    for t in range(32):
        wg_ref[t * 16 : t * 16 + 16, :] = w3[t]
    group_wait(S3, s3, group_recv)
    sf_ref[...] = s3[...]


def last_kernel(
    ag_any, sf_any, wg_any, ag_out, lw_ref, lb_ref, rw_ref, rb_ref, gain_ref, shift_ref, ow_ref, sf, wg, sems
):
    moves = [
        pltpu.make_async_copy(src, dst, sems.at[n])
        for n, (src, dst) in enumerate(((wg_any, wg), (sf_any, sf), (ag_any, ag_out)))
    ]
    for move in moves:
        move.start()
    moves[0].wait()
    for d in range(32):
        tile = wg[d // 2 * 32 : d // 2 * 32 + 32, d % 2 * 128 : d % 2 * 128 + 128]
        ow_ref[pl.ds(d, 32, stride=32), :] = tile.astype(F32)
    moves[1].wait()
    upper = lax.broadcasted_iota(jnp.int32, (8, 128), 0) < 4
    for t in range(16):
        tile = jnp.where(upper, sf[2 * t], sf[2 * t + 1])
        side, row, lane = (lw_ref, rw_ref)[t // 8], t % 8 // 2 * 8, t % 2 * 128
        side[row : row + 8, lane : lane + 128] = tile
    gain_ref[:, :128] = sf[0, 4:5, :]
    gain_ref[:, 128:] = sf[1, 0:1, :]
    shift_ref[:, :128] = sf[2, 4:5, :]
    shift_ref[:, 128:] = sf[3, 0:1, :]
    lb_ref[...] = sf[4, 4:5, 0:32]
    rb_ref[...] = sf[4, 4:5, 32:64]
    moves[2].wait()


def body(
    alignment, seq_mask, residue_mask, layer_norm_gain, layer_norm_bias, left_projection_weight, left_bias,
    right_projection_weight, right_bias, out_weight, pair_grad,
):
    vmem = pl.BlockSpec(memory_space=pltpu.VMEM)
    smem = pl.BlockSpec(memory_space=pltpu.SMEM)
    v = pltpu.VMEM
    shape = jax.ShapeDtypeStruct
    scratch = [
        v((128, 128), F32),
        v((2, 1024, 128), F32),
        v((8, 128, 256), F32),
        v((8, 128, 256), BF16),
        v((8, 128, 128), F32),
        v((8, 128, 256), F32),
        v((64, 256), BF16),
        v((64, 128), F32),
        v((1024, 128), F32),
        v((512, 256), BF16),
        v((8, 32, 16, 128), BF16),
        v((4, 64, 16, 128), BF16),
        v((64, 128, 256), BF16),
        v((2048, 2048), BF16),
        v((2048, 2048), BF16),
        v((2048, 128), BF16),
        v((128, 2048), BF16),
        v((256, 128), F32),
        v((8, 256, 128), BF16),
        v((2048, 128), BF16),
        v((8, 256, 128), BF16),
        v((8, 256, 128), BF16),
        v((8, 256, 128), BF16),
        v((8, 256, 128), BF16),
        v((256, 128), F32),
        v((512, 256), F32),
        v((32, 16, 256), BF16),
        v((32, 16, 256), BF16),
        v((8, 16, 256), BF16),
        v((32, 16, 256), BF16),
        v((64, 256), F32),
        v((8, 256), F32),
        v((32, 8, 128), F32),
        v((32, 8, 128), F32),
        v((8, 8, 128), F32),
        v((32, 8, 128), F32),
        pltpu.SemaphoreType.DMA((6, 8)),
        pltpu.SemaphoreType.DMA((6, 8)),
        pltpu.SemaphoreType.DMA((6,)),
        pltpu.SemaphoreType.DMA((6,)),
        pltpu.SemaphoreType.DMA,
    ]
    ag, sf, wg = pl.pallas_call(
        main_kernel,
        out_shape=(shape((1024, 256), BF16), shape((32, 8, 128), F32), shape((512, 256), BF16)),
        in_specs=[vmem] * 3 + [smem] + [vmem] * 8,
        out_specs=(vmem,) * 3,
        scratch_shapes=scratch,
        compiler_params=pltpu.CompilerParams(
            collective_id=0, has_side_effects=True, vmem_limit_bytes=58 * 1024 * 1024
        ),
        name="pair_backward",
    )(
        alignment.reshape(1024, 256), seq_mask.reshape(1, 512), residue_mask.reshape(1, 512), residue_mask,
        layer_norm_gain.reshape(1, 256), layer_norm_bias.reshape(1, 256), left_projection_weight.T,
        left_bias.reshape(1, 32), right_projection_weight.T, right_bias.reshape(1, 32), out_weight, pair_grad,
    )
    ag, lw, lbg, rw, rbg, gain, shift, ow = pl.pallas_call(
        last_kernel,
        out_shape=(
            shape((1024, 256), BF16), shape((32, 256), F32), shape((1, 32), F32), shape((32, 256), F32),
            shape((1, 32), F32), shape((1, 256), F32), shape((1, 256), F32), shape((1024, 128), F32),
        ),
        in_specs=[pl.BlockSpec(memory_space=pl.ANY)] * 3,
        out_specs=(pl.BlockSpec(memory_space=pl.ANY),) + (vmem,) * 7,
        scratch_shapes=[v((32, 8, 128), F32), v((512, 256), BF16), pltpu.SemaphoreType.DMA((3,))],
        compiler_params=pltpu.CompilerParams(vmem_limit_bytes=58 * 1024 * 1024),
        name="lay_out",
    )(ag, sf, wg)
    return (
        ag.reshape(128, 8, 256), lw.T, lbg.reshape(32), rw.T, rbg.reshape(32), gain.reshape(256), shift.reshape(256), ow,
    )


def solution(mesh):
    placed = (P("depth", ("row", "col"), None),) + (P(),) * 9 + (P("row", "col", None),)
    return jax.shard_map(
        body,
        mesh=mesh,
        in_specs=placed,
        out_specs=(P("depth", ("row", "col"), None),) + (P(),) * 7,
        check_vma=False,
    )
```

time: 88.2 us -> 85.3 us (0.967)
  local copies, waits for them, and re-layouts: 6.44 us -> 0 us
  Pallas kernels: 80.8 us -> 84.6 us
    unnamed x12 -> x0, local copies, waits for them, and re-layouts: 6.44 us -> none
    pallas_call x2, Pallas kernels: 80.8 us -> 84.6 us  [the longest x1 66.7 us: body(): pl.pallas_call(main_kernel, out_shape=(shape((1024, 256), BF16), shape((3...]
where the time goes in v2:
time: 85.3 us; the launch traced here: 85.2 us
  Pallas kernels  84.6 us (99%)
    pallas_call x1, Pallas kernels, body(): pl.pallas_call(main_kernel, out_shape=(shape((1024, 256), BF16), shape((3...  66.7 us
    pallas_call x1, Pallas kernels, body(): pl.pallas_call(last_kernel, out_shape=(shape((1024, 256), BF16), shape((3...  17.8 us

profile of v2, /device:TPU:1, one launch (start us, length us, event | category | flops | bytes accessed | tf_op | source)
XLA Modules:
  0.0 85.2 jit_solution(6037662641698834349)
XLA Ops:
  0.6 66.7 %pair_backward.1 = (bf16[1024,256]{1,0:T(8,128)(2,1)}, f32[32,8,128]{2,1,0:T(8,128)}, bf16[512,256]{1,0:T(8,128)(2,1)}) custom-call(bf16[1024,256]{1,0:T(8,128)(2,1)} %bitcast.16, s32[1,512]{1,0:T(1,128)} %bitcast.20, s32[1,512]{1,0:T(1,128)} %bitcast.19, s32[512]{0:T(512)} %res_s.1, f32[1,256]{1,0:T(1,128)} %bitcast.21, f32[1,256]{1,0:T(1,128)} %bitcast.22, ...), custom_call_target="tpu_custom_call" | custom-call | tf_op jit(solution)/shard_map/pair_backward/pallas_call | solution.py:424
  67.4 17.8 %lay_out.1 = (bf16[1024,256]{1,0:T(8,128)(2,1)}, f32[32,256]{1,0:T(8,128)}, f32[1,32]{1,0:T(1,128)}, f32[32,256]{1,0:T(8,128)}, f32[1,32]{1,0:T(1,128)}, /*index...) custom-call(bf16[1024,256]{1,0:T(8,128)(2,1)} %get-tuple-element.19.ag_any, ...), custom_call_target="tpu_custom_call" | custom-call | tf_op jit(solution)/shard_map/lay_out/pallas_call | solution.py:439

commit v3 on v2

--- a/solution.py
+++ b/solution.py
@@ -1,3 +1,5 @@
+import functools
+
 import jax
 import jax.numpy as jnp
 from jax import lax
@@ -9,7 +11,7 @@
 MESH = pl.DeviceIdType.MESH
 NT = (((1,), (1,)), ((), ()))
 TN = (((0,), (0,)), ((), ()))
-PAIR, LEFT, RIGHT, RSUM, RSUM2, LSUM = range(6)
+PAIR, OTHER, LEFT, RIGHT, RSUM, RSUM2, LSUM = range(7)
 W1, W2, W3, S1, S2, S3 = range(6)
 
 
@@ -22,15 +24,24 @@
 
 
 def main_kernel(
-    x_ref, seq_ref, res_ref, res_s, gain_ref, shift_ref, wl_ref, lb_ref, wr_ref, rb_ref, ow_ref, pair_ref,
-    ag_ref, sf_ref, wg_ref,
-    inv1, xf, unit, norm, istd, ngrad, wt, bias, wf, wp, ps, scb, bd, og, outer, lb, lt, rf, rbuf, rt,
+    x_any, seq_ref, res_ref, res_s, gain_ref, shift_ref, wl_ref, lb_ref, wr_ref, rb_ref, ow_any, pair_any,
+    ag_any, sf_ref, wg_ref,
+    pair_ref, x_ref, ow_ref, ag_ref, inv1, xf, unit, norm, istd, ngrad, wt, bias, wf, wp, ps, scb, bd, og, outer, lb, lt, rf, rbuf, rt,
     rss, rsr, lss, lsr, lsf, wga, w1s, w1r, w2, w3, wgt, extra, s1s, s1r, s2, s3,
-    send_sem, recv_sem, group_send, group_recv, local_sem,
+    send_sem, recv_sem, group_send, group_recv, local_sems,
 ):
     depth, row, col = lax.axis_index("depth"), lax.axis_index("row"), lax.axis_index("col")
     z, h = lax.div(row, 2), lax.rem(row, 2)
     q = h * 4 + col
+    core = lax.rem(depth, 2)
+
+    loads = [
+        pltpu.make_async_copy(pair_any.at[pl.ds(core * 16, 16)], pair_ref, local_sems.at[0]),
+        pltpu.make_async_copy(x_any, x_ref, local_sems.at[1]),
+        pltpu.make_async_copy(ow_any, ow_ref, local_sems.at[2]),
+    ]
+    for load in loads:
+        load.start()
 
     def zpeer(k):
         t = lax.rem(z + k, 8)
@@ -55,22 +66,36 @@
 
     def pair_copy(k):
         t, device = qpeer(k)
-        return copy(PAIR, k, ps.at[t], scb.at[col, pl.ds(h * 32, 32)], device)
+        return copy(PAIR, k, ps.at[t], scb.at[core, col, h], device)
+
+    def other_copy(k):
+        t = lax.rem(q + 8 - k, 8)
+        block = scb.at[core, lax.rem(t, 4), lax.div(t, 4)]
+        return copy(OTHER, k, block, block, (depth + 1 - 2 * core, row, col))
 
     def left_copy(k):
         block = lb.at[pl.ds(pl.multiple_of(q * 256, 256), 256)]
         return copy(LEFT, k, block, block, qpeer(k)[1])
 
-    def right_copy(k):
-        return copy(RIGHT, k, rbuf.at[z], rbuf.at[z], zpeer(k)[1])
-
-    def rsum_copy(k, part=0):
-        t, device = zpeer(k)
+    def right_copy(n):
+        to = (1, 7, 2, 6, 7, 1, 6, 2)[n]
+        whose = (0, 0, 0, 0, 2, 6, 2, 6)[n]
+        block = rbuf.at[lax.rem(z + whose, 8)]
+        if n >= 6:
+            block = block.at[pl.ds((n - 6) * 128, 128)]
+        return copy(RIGHT, n, block, block, zpeer(to)[1])
+
+    def rsum_copy(n, part):
+        to = (1, 7, 1, 7, 2, 6)[n]
+        whose = (1, 7, 3, 5, 4, 4)[n]
         half = pl.ds(part * 128, 128)
-        return copy(RSUM + part, k, rss.at[t, half], rsr.at[k, half], device)
-
-    def rsum2_copy(k):
-        return rsum_copy(k, 1)
+        return copy(RSUM + part, n, rss.at[lax.rem(z + whose, 8), half], rsr.at[n, half], zpeer(to)[1])
+
+    def rsum_late(n):
+        return copy(RSUM, n, rsr.at[n + 2], rsr.at[n], zpeer((2, 6)[n - 6])[1])
+
+    def rsum_all(part):
+        return [functools.partial(rsum_copy, n, part) for n in (2, 3, 4 + part, 0, 1)]
 
     def lsum_copy(k):
         t, device = qpeer(k)
@@ -117,14 +142,15 @@
     def _(k):
         pl.semaphore_signal(barrier, inc=1, device_id=gpeer(k)[1], device_id_type=MESH)
 
+    loads[0].wait()
     used = jnp.sum(seq_ref[...].astype(F32), axis=1, keepdims=True)
     res_j = res_ref[:, pl.ds(pl.multiple_of(col * 128, 128), 128)].astype(F32)
     res_j = jnp.broadcast_to(res_j, (128, 128)).T
     inv1[...] = 1.0 / jnp.maximum(used * res_j, 1.0)
 
-    @pl.loop(0, 32)
+    @pl.loop(0, 16, unroll=2)
     def _(i):
-        res_i = res_s[row * 32 + i].astype(F32)
+        res_i = res_s[row * 32 + core * 16 + i].astype(F32)
         scaled = pair_ref[i].astype(F32) * (inv1[...] * res_i + (1.0 - res_i))
         for t in range(8):
             piece = jnp.concatenate([scaled[t * 8 : t * 8 + 8], scaled[64 + t * 8 : 72 + t * 8]], axis=0)
@@ -132,7 +158,7 @@
 
     pl.semaphore_wait(barrier, 38)
     start(pair_copy)
-    own_pair = pltpu.make_async_copy(ps.at[q], scb.at[col, pl.ds(h * 32, 32)], local_sem)
+    own_pair = pltpu.make_async_copy(ps.at[q], scb.at[core, col, h], local_sems.at[3])
     own_pair.start()
 
     pick = lax.broadcasted_iota(jnp.int32, (64, 32), 0) - lax.broadcasted_iota(jnp.int32, (64, 32), 1)
@@ -143,6 +169,7 @@
     bias[...] = dot_nt(first, jnp.broadcast_to(lb_ref[...], (128, 32)), **exact) + dot_nt(
         second, jnp.broadcast_to(rb_ref[...], (128, 32)), **exact
     )
+    loads[1].wait()
     for e in range(2):
         xf[e] = x_ref[:, e * 128 : e * 128 + 128].astype(F32)
     seq_row = seq_ref[:, pl.ds(pl.multiple_of(depth * 128, 128), 128)].astype(F32)
@@ -164,9 +191,11 @@
         rf[pl.ds(r, 32, stride=8), :] = both[32:]
 
     rbuf[z] = rf[...].astype(BF16)
+    for n in (2, 3, 0, 1):
+        right_copy(n).start()
     start(left_copy)
-    start(right_copy)
-
+
+    loads[2].wait()
     wf[...] = ow_ref[...].astype(F32)
     for d in range(32):
         wp[d // 2 * 32 : d // 2 * 32 + 32, d % 2 * 128 : d % 2 * 128 + 128] = wf[pl.ds(d, 32, stride=32), :].astype(BF16)
@@ -176,19 +205,34 @@
         bd[i] = jnp.zeros((128, 256), BF16)
 
     own_pair.wait()
-    arrived(pair_copy)
-
-    @pl.loop(0, 32, unroll=8)
-    def _(t):
-        for e in range(2):
-            block = jnp.concatenate([scb[y, 2 * t + e] for y in range(4)], axis=0)
-            bd[2 * t + e, :64, :128] = block
-            bd[2 * t + e, 64:, 128:] = block
-        grads = dot_nt(wp[...], bd[pl.ds(2 * t, 2)].reshape(256, 256)).astype(BF16)
-        for e in range(2):
-            at = pl.ds(pl.multiple_of((2 * t + e) * 32, 32), 32)
-            for p in range(16):
-                og[at, p * 128 : p * 128 + 128] = grads[p * 32 : p * 32 + 32, e * 128 : e * 128 + 128]
+    other_copy(0).start()
+    for n in (2, 3):
+        right_copy(n).wait_recv()
+    for n in (4, 5, 6, 7):
+        right_copy(n).start()
+    for k in range(1, 8):
+        pair_copy(k).wait_recv()
+        other_copy(k).start()
+
+    def outer_grads(side):
+        @pl.loop(0, 16, unroll=8)
+        def _(t):
+            upper, at = lax.div(t, 8), lax.rem(t, 8) * 2
+            i = upper * 32 + side * 16 + at
+            for e in range(2):
+                block = jnp.concatenate([scb[side, y, upper, at + e] for y in range(4)], axis=0)
+                bd[i + e, :64, :128] = block
+                bd[i + e, 64:, 128:] = block
+            grads = dot_nt(wp[...], bd[pl.ds(i, 2)].reshape(256, 256)).astype(BF16)
+            for e in range(2):
+                rows = pl.ds(pl.multiple_of((i + e) * 32, 32), 32)
+                for p in range(16):
+                    og[rows, p * 128 : p * 128 + 128] = grads[p * 32 : p * 32 + 32, e * 128 : e * 128 + 128]
+
+    outer_grads(core)
+    for k in range(8):
+        other_copy(k).wait_recv()
+    outer_grads(1 - core)
 
     arrived(left_copy)
     for t in range(16):
@@ -204,12 +248,13 @@
                 piece = jnp.concatenate([turned[t * 8 : t * 8 + 8], turned[64 + t * 8 : 72 + t * 8]], axis=0)
                 rss[t, at : at + 16, :] = piece.astype(BF16)
 
-    right_sums(0)
-    start(rsum_copy)
-    right_sums(1)
-    start(rsum2_copy)
-
-    arrived(right_copy)
+    for part in range(2):
+        right_sums(part)
+        for make in rsum_all(part):
+            make().start()
+
+    for n in (0, 1, 4, 5, 6, 7):
+        right_copy(n).wait_recv()
 
     @pl.loop(0, 16)
     def _(p):
@@ -227,6 +272,15 @@
         lsum_copy(k).start()
 
     left_sum(q)
+
+    for part in range(2):
+        for make in rsum_all(part)[:3]:
+            make().wait_recv()
+    for n in range(2):
+        half = pl.ds(n * 128, 128)
+        rsr[8 + n] = (rss[lax.rem(z + (2, 6)[n], 8)].astype(F32) + rsr[2 + n].astype(F32)).astype(BF16)
+        rsr[8 + n, half] = (rsr[8 + n, half].astype(F32) + rsr[4 + n, half].astype(F32)).astype(BF16)
+        rsum_late(6 + n).start()
 
     @pl.loop(0, 8, unroll=4)
     def _(n):
@@ -254,11 +308,14 @@
     for k in range(1, 8):
         total = total + lsr[k].astype(F32)
     lsf[...] = total
-    arrived(rsum_copy)
-    arrived(rsum2_copy)
+    for part in range(2):
+        for make in rsum_all(part)[3:]:
+            make().wait_recv()
     total = rss[z].astype(F32)
-    for k in range(1, 8):
-        total = total + rsr[k].astype(F32)
+    for n in (0, 1, 6, 7):
+        if n >= 6:
+            rsum_late(n).wait_recv()
+        total = total + rsr[n].astype(F32)
     rf[...] = total
 
     wgt[...] = jnp.zeros_like(wgt)
@@ -321,6 +378,8 @@
 
     for e in range(2):
         ag_ref[:, e * 128 : e * 128 + 128] = xf[e].astype(BF16)
+    store = pltpu.make_async_copy(ag_ref, ag_any, local_sems.at[4])
+    store.start()
 
     group_wait(W2, w2, group_recv)
     w3[g] = summed(w2, 8, w2[0].astype(F32)).astype(BF16)
@@ -329,9 +388,16 @@
     s3[g] = summed(s2, 8, s2[0])
     gather_plane(S3, s3)
 
-    for make in (pair_copy, left_copy, right_copy, rsum_copy, rsum2_copy, lsum_copy):
+    for make in (pair_copy, left_copy, lsum_copy):
         for k in range(1, 8):
             make(k).wait_send()
+    for n in range(8):
+        other_copy(n).wait_send()
+        right_copy(n).wait_send()
+    for make in rsum_all(0) + rsum_all(1):
+        make().wait_send()
+    for n in (6, 7):
+        rsum_late(n).wait_send()
     for which, ref in ((W1, w1s), (W2, w2), (W3, w3), (S1, s1s), (S2, s2), (S3, s3)):
         group_wait(which, ref, group_send)
 
@@ -340,22 +406,25 @@
         wg_ref[t * 16 : t * 16 + 16, :] = w3[t]
     group_wait(S3, s3, group_recv)
     sf_ref[...] = s3[...]
+    store.wait()
 
 
 def last_kernel(
-    ag_any, sf_any, wg_any, ag_out, lw_ref, lb_ref, rw_ref, rb_ref, gain_ref, shift_ref, ow_ref, sf, wg, sems
+    ag_any, sf_any, wg_any, ag_out, lw_ref, lb_ref, rw_ref, rb_ref, gain_ref, shift_ref, ow_ref, sf, wg, ag, sems
 ):
     moves = [
         pltpu.make_async_copy(src, dst, sems.at[n])
-        for n, (src, dst) in enumerate(((wg_any, wg), (sf_any, sf), (ag_any, ag_out)))
+        for n, (src, dst) in enumerate(((ag_any, ag), (wg_any, wg), (sf_any, sf), (ag, ag_out)))
     ]
-    for move in moves:
+    for move in moves[:3]:
         move.start()
     moves[0].wait()
+    moves[3].start()
+    moves[1].wait()
     for d in range(32):
         tile = wg[d // 2 * 32 : d // 2 * 32 + 32, d % 2 * 128 : d % 2 * 128 + 128]
         ow_ref[pl.ds(d, 32, stride=32), :] = tile.astype(F32)
-    moves[1].wait()
+    moves[2].wait()
     upper = lax.broadcasted_iota(jnp.int32, (8, 128), 0) < 4
     for t in range(16):
         tile = jnp.where(upper, sf[2 * t], sf[2 * t + 1])
@@ -367,7 +436,7 @@
     shift_ref[:, 128:] = sf[3, 0:1, :]
     lb_ref[...] = sf[4, 4:5, 0:32]
     rb_ref[...] = sf[4, 4:5, 32:64]
-    moves[2].wait()
+    moves[3].wait()
 
 
 def body(
@@ -376,9 +445,14 @@
 ):
     vmem = pl.BlockSpec(memory_space=pltpu.VMEM)
     smem = pl.BlockSpec(memory_space=pltpu.SMEM)
+    hbm = pl.BlockSpec(memory_space=pl.ANY)
     v = pltpu.VMEM
     shape = jax.ShapeDtypeStruct
     scratch = [
+        v((16, 128, 128), BF16),
+        v((1024, 256), BF16),
+        v((1024, 128), BF16),
+        v((1024, 256), BF16),
         v((128, 128), F32),
         v((2, 1024, 128), F32),
         v((8, 128, 256), F32),
@@ -389,8 +463,8 @@
         v((64, 128), F32),
         v((1024, 128), F32),
         v((512, 256), BF16),
-        v((8, 32, 16, 128), BF16),
-        v((4, 64, 16, 128), BF16),
+        v((8, 16, 16, 128), BF16),
+        v((2, 4, 2, 16, 16, 128), BF16),
         v((64, 128, 256), BF16),
         v((2048, 2048), BF16),
         v((2048, 2048), BF16),
@@ -400,7 +474,7 @@
         v((8, 256, 128), BF16),
         v((2048, 128), BF16),
         v((8, 256, 128), BF16),
-        v((8, 256, 128), BF16),
+        v((10, 256, 128), BF16),
         v((8, 256, 128), BF16),
         v((8, 256, 128), BF16),
         v((256, 128), F32),
@@ -415,17 +489,17 @@
         v((32, 8, 128), F32),
         v((8, 8, 128), F32),
         v((32, 8, 128), F32),
-        pltpu.SemaphoreType.DMA((6, 8)),
-        pltpu.SemaphoreType.DMA((6, 8)),
+        pltpu.SemaphoreType.DMA((7, 8)),
+        pltpu.SemaphoreType.DMA((7, 8)),
         pltpu.SemaphoreType.DMA((6,)),
         pltpu.SemaphoreType.DMA((6,)),
-        pltpu.SemaphoreType.DMA,
+        pltpu.SemaphoreType.DMA((5,)),
     ]
     ag, sf, wg = pl.pallas_call(
         main_kernel,
         out_shape=(shape((1024, 256), BF16), shape((32, 8, 128), F32), shape((512, 256), BF16)),
-        in_specs=[vmem] * 3 + [smem] + [vmem] * 8,
-        out_specs=(vmem,) * 3,
+        in_specs=[hbm] + [vmem] * 2 + [smem] + [vmem] * 6 + [hbm] * 2,
+        out_specs=(hbm, vmem, vmem),
         scratch_shapes=scratch,
         compiler_params=pltpu.CompilerParams(
             collective_id=0, has_side_effects=True, vmem_limit_bytes=58 * 1024 * 1024
@@ -444,7 +518,7 @@
         ),
         in_specs=[pl.BlockSpec(memory_space=pl.ANY)] * 3,
         out_specs=(pl.BlockSpec(memory_space=pl.ANY),) + (vmem,) * 7,
-        scratch_shapes=[v((32, 8, 128), F32), v((512, 256), BF16), pltpu.SemaphoreType.DMA((3,))],
+        scratch_shapes=[v((32, 8, 128), F32), v((512, 256), BF16), v((1024, 256), BF16), pltpu.SemaphoreType.DMA((4,))],
         compiler_params=pltpu.CompilerParams(vmem_limit_bytes=58 * 1024 * 1024),
         name="lay_out",
     )(ag, sf, wg)

time: 85.3 us -> 63.5 us (0.74)
  Pallas kernels: 84.6 us -> 62.6 us
    pallas_call x1, Pallas kernels: 17.8 us -> 2.7 us  [body(): pl.pallas_call(last_kernel, out_shape=(shape((1024, 256), BF16), shape((3...]
    pallas_call x1, Pallas kernels: 66.7 us -> 59.9 us  [body(): pl.pallas_call(main_kernel, out_shape=(shape((1024, 256), BF16), shape((3...]
where the time goes in v3:
time: 63.5 us; the launch traced here: 63.3 us
  Pallas kernels  62.6 us (99%)
  between operations  0.65 us (1%)
    pallas_call x1, Pallas kernels, body(): pl.pallas_call(main_kernel, out_shape=(shape((1024, 256), BF16), shape((3...  59.9 us
    pallas_call x1, Pallas kernels, body(): pl.pallas_call(last_kernel, out_shape=(shape((1024, 256), BF16), shape((3...  2.7 us

profile of v3, /device:TPU:1, one launch (start us, length us, event | category | flops | bytes accessed | tf_op | source)
XLA Modules:
  0.0 63.3 jit_solution(8397863953175712452)
XLA Ops:
  0.6 59.9 %pair_backward.1 = (bf16[1024,256]{1,0:T(8,128)(2,1)}, f32[32,8,128]{2,1,0:T(8,128)}, bf16[512,256]{1,0:T(8,128)(2,1)}) custom-call(bf16[1024,256]{1,0:T(8,128)(2,1)} %bitcast.16, s32[1,512]{1,0:T(1,128)} %bitcast.20, s32[1,512]{1,0:T(1,128)} %bitcast.19, s32[512]{0:T(512)} %res_s.1, f32[1,256]{1,0:T(1,128)} %bitcast.21, f32[1,256]{1,0:T(1,128)} %bitcast.22, ...), custom_call_target="tpu_custom_call" | custom-call | tf_op jit(solution)/shard_map/pair_backward/pallas_call | solution.py:498
  60.6 2.7 %lay_out.1 = (bf16[1024,256]{1,0:T(8,128)(2,1)}, f32[32,256]{1,0:T(8,128)}, f32[1,32]{1,0:T(1,128)}, f32[32,256]{1,0:T(8,128)}, f32[1,32]{1,0:T(1,128)}, /*index...) custom-call(bf16[1024,256]{1,0:T(8,128)(2,1)} %get-tuple-element.19.ag_any, ...), custom_call_target="tpu_custom_call" | custom-call | tf_op jit(solution)/shard_map/lay_out/pallas_call | solution.py:513

commit v4 on v3

--- a/solution.py
+++ b/solution.py
@@ -25,7 +25,7 @@
 
 def main_kernel(
     x_any, seq_ref, res_ref, res_s, gain_ref, shift_ref, wl_ref, lb_ref, wr_ref, rb_ref, ow_any, pair_any,
-    ag_any, sf_ref, wg_ref,
+    ag_any, sf_any, wg_any,
     pair_ref, x_ref, ow_ref, ag_ref, inv1, xf, unit, norm, istd, ngrad, wt, bias, wf, wp, ps, scb, bd, og, outer, lb, lt, rf, rbuf, rt,
     rss, rsr, lss, lsr, lsf, wga, w1s, w1r, w2, w3, wgt, extra, s1s, s1r, s2, s3,
     send_sem, recv_sem, group_send, group_recv, local_sems,
@@ -53,10 +53,17 @@
 
     g = depth * 8 + q
 
+    steps = sorted(
+        [(n // 16, n // 8 % 2, n // 4 % 2, n % 4) for n in range(1, 32)],
+        key=lambda step: -(step[0] + (0, 2, 1, 1)[step[1] + 2 * step[2]] + (0, 1, 2, 1)[step[3]]),
+    )
+
     def gpeer(k):
-        t = lax.rem(g + k, 32)
-        u = lax.rem(t, 8)
-        return t, (lax.div(t, 8), z * 2 + lax.div(u, 4), lax.rem(u, 4))
+        side, over, low, along = steps[k - 1]
+        to_core, to_low = lax.rem(core + side, 2), lax.rem(lax.div(depth, 2) + low, 2)
+        to_h, to_col = lax.rem(h + over, 2), lax.rem(col + along, 4)
+        to_depth = to_low * 2 + to_core
+        return to_depth * 8 + to_h * 4 + to_col, (to_depth, z * 2 + to_h, to_col)
 
     def copy(which, k, src, dst, device):
         return pltpu.make_async_remote_copy(
@@ -91,8 +98,9 @@
         half = pl.ds(part * 128, 128)
         return copy(RSUM + part, n, rss.at[lax.rem(z + whose, 8), half], rsr.at[n, half], zpeer(to)[1])
 
-    def rsum_late(n):
-        return copy(RSUM, n, rsr.at[n + 2], rsr.at[n], zpeer((2, 6)[n - 6])[1])
+    def rsum_late(n, part):
+        half = pl.ds(part * 128, 128)
+        return copy(RSUM + part, n, rsr.at[n + 2, half], rsr.at[n, half], zpeer((2, 6)[n - 6])[1])
 
     def rsum_all(part):
         return [functools.partial(rsum_copy, n, part) for n in (2, 3, 4 + part, 0, 1)]
@@ -108,18 +116,16 @@
         )
 
     def scatter_plane(which, src, dst):
-        @pl.loop(1, 32)
-        def _(k):
+        for k in range(1, 32):
             t, device = gpeer(k)
             group_copy(which, src.at[t], dst.at[k], device).start()
 
     def share_line(which, ref):
-        for k in range(1, 8):
+        for k in (4, 3, 5, 2, 6, 1, 7):
             group_copy(which, ref.at[z], ref.at[z], zpeer(k)[1]).start()
 
     def gather_plane(which, ref):
-        @pl.loop(1, 32)
-        def _(k):
+        for k in range(1, 32):
             group_copy(which, ref.at[g], ref.at[g], gpeer(k)[1]).start()
 
     def group_wait(which, ref, sems):
@@ -138,8 +144,7 @@
     for k in range(1, 8):
         pl.semaphore_signal(barrier, inc=1, device_id=zpeer(k)[1], device_id_type=MESH)
 
-    @pl.loop(1, 32)
-    def _(k):
+    for k in range(1, 32):
         pl.semaphore_signal(barrier, inc=1, device_id=gpeer(k)[1], device_id_type=MESH)
 
     loads[0].wait()
@@ -234,10 +239,28 @@
         other_copy(k).wait_recv()
     outer_grads(1 - core)
 
-    arrived(left_copy)
-    for t in range(16):
-        block = lb[t * 128 : t * 128 + 128, :].astype(F32)
-        lt[:, t * 128 : t * 128 + 128] = block.T.astype(BF16)
+    for n in (0, 1, 4, 5, 6, 7):
+        right_copy(n).wait_recv()
+
+    @pl.loop(0, 16, unroll=4)
+    def _(p):
+        blocks = [rbuf[t, pl.ds(pl.multiple_of(p * 16, 16), 16), :].astype(F32) for t in range(8)]
+        rows = [block[:8] for block in blocks] + [block[8:] for block in blocks]
+        rt[pl.ds(pl.multiple_of(p * 128, 128), 128), :] = jnp.concatenate(rows, axis=0).astype(BF16)
+
+    def products(t):
+        at = pl.multiple_of(t * 256, 256)
+        block = lb[pl.ds(at, 256), :]
+        outer[pl.ds(at, 256), :] = dot_nt(block, rt[...]).astype(BF16)
+        for e in range(2):
+            lt[:, pl.ds(at + e * 128, 128)] = block[e * 128 : e * 128 + 128].astype(F32).T.astype(BF16)
+
+    products(q)
+
+    @pl.loop(1, 8)
+    def _(k):
+        left_copy(k).wait_recv()
+        products(lax.rem(q + 8 - k, 8))
 
     def right_sums(part):
         sums = dot(lt[...], og[:, part * 1024 : part * 1024 + 1024])
@@ -250,44 +273,43 @@
 
     for part in range(2):
         right_sums(part)
-        for make in rsum_all(part):
+        for make in rsum_all(part)[:3]:
             make().start()
-
-    for n in (0, 1, 4, 5, 6, 7):
-        right_copy(n).wait_recv()
-
-    @pl.loop(0, 16)
-    def _(p):
-        blocks = [rbuf[t, pl.ds(pl.multiple_of(p * 16, 16), 16), :].astype(F32) for t in range(8)]
-        rows = [block[:8] for block in blocks] + [block[8:] for block in blocks]
-        rt[pl.ds(pl.multiple_of(p * 128, 128), 128), :] = jnp.concatenate(rows, axis=0).astype(BF16)
+    for part in range(2):
+        for make in rsum_all(part)[3:]:
+            make().start()
 
     def left_sum(t):
         at = pl.ds(pl.multiple_of(t * 256, 256), 256)
         lss[t] = dot(og[at, :], rt[...]).astype(BF16)
 
-    @pl.loop(1, 8)
-    def _(k):
+    def send_left(k):
         left_sum(lax.rem(q + k, 8))
         lsum_copy(k).start()
 
-    left_sum(q)
-
-    for part in range(2):
+    def relay(part):
+        half = pl.ds(part * 128, 128)
         for make in rsum_all(part)[:3]:
             make().wait_recv()
-    for n in range(2):
-        half = pl.ds(n * 128, 128)
-        rsr[8 + n] = (rss[lax.rem(z + (2, 6)[n], 8)].astype(F32) + rsr[2 + n].astype(F32)).astype(BF16)
-        rsr[8 + n, half] = (rsr[8 + n, half].astype(F32) + rsr[4 + n, half].astype(F32)).astype(BF16)
-        rsum_late(6 + n).start()
-
-    @pl.loop(0, 8, unroll=4)
-    def _(n):
-        at = pl.ds(pl.multiple_of(n * 256, 256), 256)
-        for m in range(4):
-            product = dot_nt(lb[m * 512 : m * 512 + 512, :], rt[at, :])
-            outer[m * 512 : m * 512 + 512, at] = product.astype(BF16)
+        for n in range(2):
+            total = rss[lax.rem(z + (2, 6)[n], 8), half].astype(F32) + rsr[2 + n, half].astype(F32)
+            if n == part:
+                total = total + rsr[4 + n, half].astype(F32)
+            rsr[8 + n, half] = total.astype(BF16)
+            rsum_late(6 + n, part).start()
+
+    @pl.loop(1, 5)
+    def _(k):
+        send_left(k)
+
+    relay(0)
+
+    @pl.loop(5, 8)
+    def _(k):
+        send_left(k)
+
+    relay(1)
+    left_sum(q)
 
     wga[...] = jnp.zeros_like(wga)
 
@@ -314,7 +336,8 @@
     total = rss[z].astype(F32)
     for n in (0, 1, 6, 7):
         if n >= 6:
-            rsum_late(n).wait_recv()
+            rsum_late(n, 0).wait_recv()
+            rsum_late(n, 1).wait_recv()
         total = total + rsr[n].astype(F32)
     rf[...] = total
 
@@ -397,16 +420,20 @@
     for make in rsum_all(0) + rsum_all(1):
         make().wait_send()
     for n in (6, 7):
-        rsum_late(n).wait_send()
+        rsum_late(n, 0).wait_send()
+        rsum_late(n, 1).wait_send()
     for which, ref in ((W1, w1s), (W2, w2), (W3, w3), (S1, s1s), (S2, s2), (S3, s3)):
         group_wait(which, ref, group_send)
 
     group_wait(W3, w3, group_recv)
-    for t in range(32):
-        wg_ref[t * 16 : t * 16 + 16, :] = w3[t]
+    store_wg = pltpu.make_async_copy(w3, wg_any, local_sems.at[0])
+    store_wg.start()
     group_wait(S3, s3, group_recv)
-    sf_ref[...] = s3[...]
+    store_sf = pltpu.make_async_copy(s3, sf_any, local_sems.at[1])
+    store_sf.start()
     store.wait()
+    store_wg.wait()
+    store_sf.wait()
 
 
 def last_kernel(
@@ -422,7 +449,7 @@
     moves[3].start()
     moves[1].wait()
     for d in range(32):
-        tile = wg[d // 2 * 32 : d // 2 * 32 + 32, d % 2 * 128 : d % 2 * 128 + 128]
+        tile = wg[d // 2 * 2 : d // 2 * 2 + 2, :, d % 2 * 128 : d % 2 * 128 + 128].reshape(32, 128)
         ow_ref[pl.ds(d, 32, stride=32), :] = tile.astype(F32)
     moves[2].wait()
     upper = lax.broadcasted_iota(jnp.int32, (8, 128), 0) < 4
@@ -497,9 +524,9 @@
     ]
     ag, sf, wg = pl.pallas_call(
         main_kernel,
-        out_shape=(shape((1024, 256), BF16), shape((32, 8, 128), F32), shape((512, 256), BF16)),
+        out_shape=(shape((1024, 256), BF16), shape((32, 8, 128), F32), shape((32, 16, 256), BF16)),
         in_specs=[hbm] + [vmem] * 2 + [smem] + [vmem] * 6 + [hbm] * 2,
-        out_specs=(hbm, vmem, vmem),
+        out_specs=(hbm,) * 3,
         scratch_shapes=scratch,
         compiler_params=pltpu.CompilerParams(
             collective_id=0, has_side_effects=True, vmem_limit_bytes=58 * 1024 * 1024
@@ -518,7 +545,7 @@
         ),
         in_specs=[pl.BlockSpec(memory_space=pl.ANY)] * 3,
         out_specs=(pl.BlockSpec(memory_space=pl.ANY),) + (vmem,) * 7,
-        scratch_shapes=[v((32, 8, 128), F32), v((512, 256), BF16), v((1024, 256), BF16), pltpu.SemaphoreType.DMA((4,))],
+        scratch_shapes=[v((32, 8, 128), F32), v((32, 16, 256), BF16), v((1024, 256), BF16), pltpu.SemaphoreType.DMA((4,))],
         compiler_params=pltpu.CompilerParams(vmem_limit_bytes=58 * 1024 * 1024),
         name="lay_out",
     )(ag, sf, wg)

time: 63.5 us -> 64.6 us (1.017)
  Pallas kernels: 62.6 us -> 63.8 us
    pallas_call x1, Pallas kernels: 59.9 us -> 61.1 us  [body(): pl.pallas_call(main_kernel, out_shape=(shape((1024, 256), BF16), shape((3...]
where the time goes in v4:
time: 64.6 us; the launch traced here: 64.4 us
  Pallas kernels  63.8 us (99%)
  between operations  0.65 us (1%)
    pallas_call x1, Pallas kernels, body(): pl.pallas_call(main_kernel, out_shape=(shape((1024, 256), BF16), shape((3...  61.1 us
    pallas_call x1, Pallas kernels, body(): pl.pallas_call(last_kernel, out_shape=(shape((1024, 256), BF16), shape((3...  2.7 us

profile of v4, /device:TPU:1, one launch (start us, length us, event | category | flops | bytes accessed | tf_op | source)
XLA Modules:
  0.0 64.4 jit_solution(3709795603979853405)
XLA Ops:
  0.6 61.1 %pair_backward.1 = (bf16[1024,256]{1,0:T(8,128)(2,1)}, f32[32,8,128]{2,1,0:T(8,128)}, bf16[32,16,256]{2,1,0:T(8,128)(2,1)}) custom-call(bf16[1024,256]{1,0:T(8,128)(2,1)} %bitcast.16, s32[1,512]{1,0:T(1,128)} %bitcast.20, s32[1,512]{1,0:T(1,128)} %bitcast.19, s32[512]{0:T(512)} %res_s.1, f32[1,256]{1,0:T(1,128)} %bitcast.21, f32[1,256]{1,0:T(1,128)} %bitcast.22, ...), custom_call_target="tpu_custom_call" | custom-call | tf_op jit(solution)/shard_map/pair_backward/pallas_call | solution.py:525
  61.7 2.7 %lay_out.1 = (bf16[1024,256]{1,0:T(8,128)(2,1)}, f32[32,256]{1,0:T(8,128)}, f32[1,32]{1,0:T(1,128)}, f32[32,256]{1,0:T(8,128)}, f32[1,32]{1,0:T(1,128)}, /*index...) custom-call(bf16[1024,256]{1,0:T(8,128)(2,1)} %get-tuple-element.19.ag_any, ...), custom_call_target="tpu_custom_call" | custom-call | tf_op jit(solution)/shard_map/lay_out/pallas_call | solution.py:540

commit v5 on v4

--- a/solution.py
+++ b/solution.py
@@ -24,22 +24,24 @@
 
 
 def main_kernel(
-    x_any, seq_ref, res_ref, res_s, gain_ref, shift_ref, wl_ref, lb_ref, wr_ref, rb_ref, ow_any, pair_any,
+    x_any, seq_any, res_any, res_flat, gain_any, shift_any, wl_any, lb_any, wr_any, rb_any, ow_any, pair_any,
     ag_any, sf_any, wg_any,
-    pair_ref, x_ref, ow_ref, ag_ref, inv1, xf, unit, norm, istd, ngrad, wt, bias, wf, wp, ps, scb, bd, og, outer, lb, lt, rf, rbuf, rt,
+    pair_ref, x_ref, ow_ref, ag_ref,
+    seq_ref, res_ref, res_s, gain_ref, shift_ref, wl_ref, lb_ref, wr_ref, rb_ref, inv1, xf, unit, norm, istd, ngrad, wt, bias, wf, wp, ps, scb, bd, og, outer, lb, lt, rf, rbuf, rt,
     rss, rsr, lss, lsr, lsf, wga, w1s, w1r, w2, w3, wgt, extra, s1s, s1r, s2, s3,
-    send_sem, recv_sem, group_send, group_recv, local_sems,
+    send_sem, recv_sem, group_send, group_recv, local_sems, load_sems,
 ):
     depth, row, col = lax.axis_index("depth"), lax.axis_index("row"), lax.axis_index("col")
     z, h = lax.div(row, 2), lax.rem(row, 2)
     q = h * 4 + col
     core = lax.rem(depth, 2)
 
-    loads = [
-        pltpu.make_async_copy(pair_any.at[pl.ds(core * 16, 16)], pair_ref, local_sems.at[0]),
-        pltpu.make_async_copy(x_any, x_ref, local_sems.at[1]),
-        pltpu.make_async_copy(ow_any, ow_ref, local_sems.at[2]),
-    ]
+    moves = (
+        (pair_any.at[pl.ds(core * 16, 16)], pair_ref), (seq_any, seq_ref), (res_any, res_ref), (res_flat, res_s),
+        (x_any, x_ref), (gain_any, gain_ref), (shift_any, shift_ref), (wl_any, wl_ref), (lb_any, lb_ref),
+        (wr_any, wr_ref), (rb_any, rb_ref), (ow_any, ow_ref),
+    )
+    loads = [pltpu.make_async_copy(src, dst, load_sems.at[n]) for n, (src, dst) in enumerate(moves)]
     for load in loads:
         load.start()
 
@@ -51,19 +53,13 @@
         t = lax.rem(q + k, 8)
         return t, (depth, z * 2 + lax.div(t, 4), lax.rem(t, 4))
 
+
     g = depth * 8 + q
 
-    steps = sorted(
-        [(n // 16, n // 8 % 2, n // 4 % 2, n % 4) for n in range(1, 32)],
-        key=lambda step: -(step[0] + (0, 2, 1, 1)[step[1] + 2 * step[2]] + (0, 1, 2, 1)[step[3]]),
-    )
-
     def gpeer(k):
-        side, over, low, along = steps[k - 1]
-        to_core, to_low = lax.rem(core + side, 2), lax.rem(lax.div(depth, 2) + low, 2)
-        to_h, to_col = lax.rem(h + over, 2), lax.rem(col + along, 4)
-        to_depth = to_low * 2 + to_core
-        return to_depth * 8 + to_h * 4 + to_col, (to_depth, z * 2 + to_h, to_col)
+        t = lax.rem(g + k, 32)
+        u = lax.rem(t, 8)
+        return t, (lax.div(t, 8), z * 2 + lax.div(u, 4), lax.rem(u, 4))
 
     def copy(which, k, src, dst, device):
         return pltpu.make_async_remote_copy(
@@ -116,7 +112,8 @@
         )
 
     def scatter_plane(which, src, dst):
-        for k in range(1, 32):
+        @pl.loop(1, 32)
+        def _(k):
             t, device = gpeer(k)
             group_copy(which, src.at[t], dst.at[k], device).start()
 
@@ -125,7 +122,8 @@
             group_copy(which, ref.at[z], ref.at[z], zpeer(k)[1]).start()
 
     def gather_plane(which, ref):
-        for k in range(1, 32):
+        @pl.loop(1, 32)
+        def _(k):
             group_copy(which, ref.at[g], ref.at[g], gpeer(k)[1]).start()
 
     def group_wait(which, ref, sems):
@@ -144,10 +142,12 @@
     for k in range(1, 8):
         pl.semaphore_signal(barrier, inc=1, device_id=zpeer(k)[1], device_id_type=MESH)
 
-    for k in range(1, 32):
+    @pl.loop(1, 32)
+    def _(k):
         pl.semaphore_signal(barrier, inc=1, device_id=gpeer(k)[1], device_id_type=MESH)
 
-    loads[0].wait()
+    for load in loads[:4]:
+        load.wait()
     used = jnp.sum(seq_ref[...].astype(F32), axis=1, keepdims=True)
     res_j = res_ref[:, pl.ds(pl.multiple_of(col * 128, 128), 128)].astype(F32)
     res_j = jnp.broadcast_to(res_j, (128, 128)).T
@@ -166,6 +166,8 @@
     own_pair = pltpu.make_async_copy(ps.at[q], scb.at[core, col, h], local_sems.at[3])
     own_pair.start()
 
+    for load in loads[4:11]:
+        load.wait()
     pick = lax.broadcasted_iota(jnp.int32, (64, 32), 0) - lax.broadcasted_iota(jnp.int32, (64, 32), 1)
     first, second = (pick == 0).astype(F32), (pick == 32).astype(F32)
     wt[0:32, :] = wl_ref[...]
@@ -174,7 +176,6 @@
     bias[...] = dot_nt(first, jnp.broadcast_to(lb_ref[...], (128, 32)), **exact) + dot_nt(
         second, jnp.broadcast_to(rb_ref[...], (128, 32)), **exact
     )
-    loads[1].wait()
     for e in range(2):
         xf[e] = x_ref[:, e * 128 : e * 128 + 128].astype(F32)
     seq_row = seq_ref[:, pl.ds(pl.multiple_of(depth * 128, 128), 128)].astype(F32)
@@ -200,7 +201,7 @@
         right_copy(n).start()
     start(left_copy)
 
-    loads[2].wait()
+    loads[11].wait()
     wf[...] = ow_ref[...].astype(F32)
     for d in range(32):
         wp[d // 2 * 32 : d // 2 * 32 + 32, d % 2 * 128 : d % 2 * 128 + 128] = wf[pl.ds(d, 32, stride=32), :].astype(BF16)
@@ -239,28 +240,10 @@
         other_copy(k).wait_recv()
     outer_grads(1 - core)
 
-    for n in (0, 1, 4, 5, 6, 7):
-        right_copy(n).wait_recv()
-
-    @pl.loop(0, 16, unroll=4)
-    def _(p):
-        blocks = [rbuf[t, pl.ds(pl.multiple_of(p * 16, 16), 16), :].astype(F32) for t in range(8)]
-        rows = [block[:8] for block in blocks] + [block[8:] for block in blocks]
-        rt[pl.ds(pl.multiple_of(p * 128, 128), 128), :] = jnp.concatenate(rows, axis=0).astype(BF16)
-
-    def products(t):
-        at = pl.multiple_of(t * 256, 256)
-        block = lb[pl.ds(at, 256), :]
-        outer[pl.ds(at, 256), :] = dot_nt(block, rt[...]).astype(BF16)
-        for e in range(2):
-            lt[:, pl.ds(at + e * 128, 128)] = block[e * 128 : e * 128 + 128].astype(F32).T.astype(BF16)
-
-    products(q)
-
-    @pl.loop(1, 8)
-    def _(k):
-        left_copy(k).wait_recv()
-        products(lax.rem(q + 8 - k, 8))
+    arrived(left_copy)
+    for t in range(16):
+        block = lb[t * 128 : t * 128 + 128, :].astype(F32)
+        lt[:, t * 128 : t * 128 + 128] = block.T.astype(BF16)
 
     def right_sums(part):
         sums = dot(lt[...], og[:, part * 1024 : part * 1024 + 1024])
@@ -278,6 +261,15 @@
     for part in range(2):
         for make in rsum_all(part)[3:]:
             make().start()
+
+    for n in (0, 1, 4, 5, 6, 7):
+        right_copy(n).wait_recv()
+
+    @pl.loop(0, 16, unroll=4)
+    def _(p):
+        blocks = [rbuf[t, pl.ds(pl.multiple_of(p * 16, 16), 16), :].astype(F32) for t in range(8)]
+        rows = [block[:8] for block in blocks] + [block[8:] for block in blocks]
+        rt[pl.ds(pl.multiple_of(p * 128, 128), 128), :] = jnp.concatenate(rows, axis=0).astype(BF16)
 
     def left_sum(t):
         at = pl.ds(pl.multiple_of(t * 256, 256), 256)
@@ -298,18 +290,25 @@
             rsr[8 + n, half] = total.astype(BF16)
             rsum_late(6 + n, part).start()
 
-    @pl.loop(1, 5)
+    @pl.loop(1, 5, unroll=4)
     def _(k):
         send_left(k)
 
     relay(0)
 
-    @pl.loop(5, 8)
+    @pl.loop(5, 8, unroll=3)
     def _(k):
         send_left(k)
 
     relay(1)
     left_sum(q)
+
+    @pl.loop(0, 8, unroll=4)
+    def _(n):
+        at = pl.ds(pl.multiple_of(n * 256, 256), 256)
+        for m in range(4):
+            product = dot_nt(lb[m * 512 : m * 512 + 512, :], rt[at, :])
+            outer[m * 512 : m * 512 + 512, at] = product.astype(BF16)
 
     wga[...] = jnp.zeros_like(wga)
 
@@ -471,7 +470,6 @@
     right_projection_weight, right_bias, out_weight, pair_grad,
 ):
     vmem = pl.BlockSpec(memory_space=pltpu.VMEM)
-    smem = pl.BlockSpec(memory_space=pltpu.SMEM)
     hbm = pl.BlockSpec(memory_space=pl.ANY)
     v = pltpu.VMEM
     shape = jax.ShapeDtypeStruct
@@ -480,6 +478,15 @@
         v((1024, 256), BF16),
         v((1024, 128), BF16),
         v((1024, 256), BF16),
+        v((1, 512), jnp.int32),
+        v((1, 512), jnp.int32),
+        pltpu.SMEM((512,), jnp.int32),
+        v((1, 256), F32),
+        v((1, 256), F32),
+        v((32, 256), BF16),
+        v((1, 32), F32),
+        v((32, 256), BF16),
+        v((1, 32), F32),
         v((128, 128), F32),
         v((2, 1024, 128), F32),
         v((8, 128, 256), F32),
@@ -521,11 +528,12 @@
         pltpu.SemaphoreType.DMA((6,)),
         pltpu.SemaphoreType.DMA((6,)),
         pltpu.SemaphoreType.DMA((5,)),
+        pltpu.SemaphoreType.DMA((12,)),
     ]
     ag, sf, wg = pl.pallas_call(
         main_kernel,
         out_shape=(shape((1024, 256), BF16), shape((32, 8, 128), F32), shape((32, 16, 256), BF16)),
-        in_specs=[hbm] + [vmem] * 2 + [smem] + [vmem] * 6 + [hbm] * 2,
+        in_specs=[hbm] * 12,
         out_specs=(hbm,) * 3,
         scratch_shapes=scratch,
         compiler_params=pltpu.CompilerParams(

time: 64.6 us -> 63.3 us (0.980)
  Pallas kernels: 63.8 us -> 62.5 us
    pallas_call x1, Pallas kernels: 61.1 us -> 59.8 us  [body(): pl.pallas_call(main_kernel, out_shape=(shape((1024, 256), BF16), shape((3...]
where the time goes in v5:
time: 63.3 us; the launch traced here: 63.1 us
  Pallas kernels  62.5 us (99%)
  between operations  0.65 us (1%)
    pallas_call x1, Pallas kernels, body(): pl.pallas_call(main_kernel, out_shape=(shape((1024, 256), BF16), shape((3...  59.8 us
    pallas_call x1, Pallas kernels, body(): pl.pallas_call(last_kernel, out_shape=(shape((1024, 256), BF16), shape((3...  2.7 us

profile of v5, /device:TPU:1, one launch (start us, length us, event | category | flops | bytes accessed | tf_op | source)
XLA Modules:
  0.0 63.1 jit_solution(10135435157858185282)
XLA Ops:
  0.6 59.8 %pair_backward.1 = (bf16[1024,256]{1,0:T(8,128)(2,1)}, f32[32,8,128]{2,1,0:T(8,128)}, bf16[32,16,256]{2,1,0:T(8,128)(2,1)}) custom-call(bf16[1024,256]{1,0:T(8,128)(2,1)} %bitcast.16, s32[1,512]{1,0:T(1,128)} %bitcast.20, s32[1,512]{1,0:T(1,128)} %bitcast.19, s32[512]{0:T(512)} %res_flat.1, f32[1,256]{1,0:T(1,128)} %bitcast.21, f32[1,256]{1,0:T(1,128)} %bitcast.22, ...), custom_call_target="tpu_custom_call" | custom-call | tf_op jit(solution)/shard_map/pair_backward/pallas_call | solution.py:533
  60.4 2.7 %lay_out.1 = (bf16[1024,256]{1,0:T(8,128)(2,1)}, f32[32,256]{1,0:T(8,128)}, f32[1,32]{1,0:T(1,128)}, f32[32,256]{1,0:T(8,128)}, f32[1,32]{1,0:T(1,128)}, /*index...) custom-call(bf16[1024,256]{1,0:T(8,128)(2,1)} %get-tuple-element.19.ag_any, ...), custom_call_target="tpu_custom_call" | custom-call | tf_op jit(solution)/shard_map/lay_out/pallas_call | solution.py:548

commit v6 on v5

--- a/solution.py
+++ b/solution.py
@@ -1,5 +1,3 @@
-import functools
-
 import jax
 import jax.numpy as jnp
 from jax import lax
@@ -53,7 +51,6 @@
         t = lax.rem(q + k, 8)
         return t, (depth, z * 2 + lax.div(t, 4), lax.rem(t, 4))
 
-
     g = depth * 8 + q
 
     def gpeer(k):
@@ -80,26 +77,13 @@
         block = lb.at[pl.ds(pl.multiple_of(q * 256, 256), 256)]
         return copy(LEFT, k, block, block, qpeer(k)[1])
 
-    def right_copy(n):
-        to = (1, 7, 2, 6, 7, 1, 6, 2)[n]
-        whose = (0, 0, 0, 0, 2, 6, 2, 6)[n]
-        block = rbuf.at[lax.rem(z + whose, 8)]
-        if n >= 6:
-            block = block.at[pl.ds((n - 6) * 128, 128)]
-        return copy(RIGHT, n, block, block, zpeer(to)[1])
-
-    def rsum_copy(n, part):
-        to = (1, 7, 1, 7, 2, 6)[n]
-        whose = (1, 7, 3, 5, 4, 4)[n]
+    def right_copy(k):
+        return copy(RIGHT, k, rbuf.at[z], rbuf.at[z], zpeer(k)[1])
+
+    def rsum_copy(k, part):
+        t, device = zpeer(k)
         half = pl.ds(part * 128, 128)
-        return copy(RSUM + part, n, rss.at[lax.rem(z + whose, 8), half], rsr.at[n, half], zpeer(to)[1])
-
-    def rsum_late(n, part):
-        half = pl.ds(part * 128, 128)
-        return copy(RSUM + part, n, rsr.at[n + 2, half], rsr.at[n, half], zpeer((2, 6)[n - 6])[1])
-
-    def rsum_all(part):
-        return [functools.partial(rsum_copy, n, part) for n in (2, 3, 4 + part, 0, 1)]
+        return copy(RSUM + part, k, rss.at[t, half], rsr.at[k, half], device)
 
     def lsum_copy(k):
         t, device = qpeer(k)
@@ -197,9 +181,9 @@
         rf[pl.ds(r, 32, stride=8), :] = both[32:]
 
     rbuf[z] = rf[...].astype(BF16)
-    for n in (2, 3, 0, 1):
-        right_copy(n).start()
     start(left_copy)
+    for k in (4, 3, 5, 2, 6, 1, 7):
+        right_copy(k).start()
 
     loads[11].wait()
     wf[...] = ow_ref[...].astype(F32)
@@ -212,10 +196,6 @@
 
     own_pair.wait()
     other_copy(0).start()
-    for n in (2, 3):
-        right_copy(n).wait_recv()
-    for n in (4, 5, 6, 7):
-        right_copy(n).start()
     for k in range(1, 8):
         pair_copy(k).wait_recv()
         other_copy(k).start()
@@ -256,14 +236,10 @@
 
     for part in range(2):
         right_sums(part)
-        for make in rsum_all(part)[:3]:
-            make().start()
-    for part in range(2):
-        for make in rsum_all(part)[3:]:
-            make().start()
-
-    for n in (0, 1, 4, 5, 6, 7):
-        right_copy(n).wait_recv()
+        for k in (4, 3, 5, 2, 6, 1, 7):
+            rsum_copy(k, part).start()
+
+    arrived(right_copy)
 
     @pl.loop(0, 16, unroll=4)
     def _(p):
@@ -279,28 +255,10 @@
         left_sum(lax.rem(q + k, 8))
         lsum_copy(k).start()
 
-    def relay(part):
-        half = pl.ds(part * 128, 128)
-        for make in rsum_all(part)[:3]:
-            make().wait_recv()
-        for n in range(2):
-            total = rss[lax.rem(z + (2, 6)[n], 8), half].astype(F32) + rsr[2 + n, half].astype(F32)
-            if n == part:
-                total = total + rsr[4 + n, half].astype(F32)
-            rsr[8 + n, half] = total.astype(BF16)
-            rsum_late(6 + n, part).start()
-
-    @pl.loop(1, 5, unroll=4)
+    @pl.loop(1, 8)
     def _(k):
         send_left(k)
 
-    relay(0)
-
-    @pl.loop(5, 8, unroll=3)
-    def _(k):
-        send_left(k)
-
-    relay(1)
     left_sum(q)
 
     @pl.loop(0, 8, unroll=4)
@@ -329,15 +287,11 @@
     for k in range(1, 8):
         total = total + lsr[k].astype(F32)
     lsf[...] = total
-    for part in range(2):
-        for make in rsum_all(part)[3:]:
-            make().wait_recv()
     total = rss[z].astype(F32)
-    for n in (0, 1, 6, 7):
-        if n >= 6:
-            rsum_late(n, 0).wait_recv()
-            rsum_late(n, 1).wait_recv()
-        total = total + rsr[n].astype(F32)
+    for k in range(1, 8):
+        rsum_copy(k, 0).wait_recv()
+        rsum_copy(k, 1).wait_recv()
+        total = total + rsr[k].astype(F32)
     rf[...] = total
 
     wgt[...] = jnp.zeros_like(wgt)
@@ -415,12 +369,11 @@
             make(k).wait_send()
     for n in range(8):
         other_copy(n).wait_send()
-        right_copy(n).wait_send()
-    for make in rsum_all(0) + rsum_all(1):
-        make().wait_send()
-    for n in (6, 7):
-        rsum_late(n, 0).wait_send()
-        rsum_late(n, 1).wait_send()
+    for k in range(1, 8):
+        right_copy(k).wait_send()
+    for k in range(1, 8):
+        rsum_copy(k, 0).wait_send()
+        rsum_copy(k, 1).wait_send()
     for which, ref in ((W1, w1s), (W2, w2), (W3, w3), (S1, s1s), (S2, s2), (S3, s3)):
         group_wait(which, ref, group_send)
 
@@ -508,7 +461,7 @@
         v((8, 256, 128), BF16),
         v((2048, 128), BF16),
         v((8, 256, 128), BF16),
-        v((10, 256, 128), BF16),
+        v((8, 256, 128), BF16),
         v((8, 256, 128), BF16),
         v((8, 256, 128), BF16),
         v((256, 128), F32),

time: 63.3 us -> 61.9 us (0.978)
  Pallas kernels: 62.5 us -> 61.1 us
    pallas_call x1, Pallas kernels: 59.8 us -> 58.4 us  [body(): pl.pallas_call(main_kernel, out_shape=(shape((1024, 256), BF16), shape((3...]
where the time goes in v6:
time: 61.9 us; the launch traced here: 61.8 us
  Pallas kernels  61.1 us (99%)
  between operations  0.65 us (1%)
    pallas_call x1, Pallas kernels, body(): pl.pallas_call(main_kernel, out_shape=(shape((1024, 256), BF16), shape((3...  58.4 us
    pallas_call x1, Pallas kernels, body(): pl.pallas_call(last_kernel, out_shape=(shape((1024, 256), BF16), shape((3...  2.7 us

profile of v6, /device:TPU:1, one launch (start us, length us, event | category | flops | bytes accessed | tf_op | source)
XLA Modules:
  0.0 61.8 jit_solution(9584225155166963407)
XLA Ops:
  0.6 58.4 %pair_backward.1 = (bf16[1024,256]{1,0:T(8,128)(2,1)}, f32[32,8,128]{2,1,0:T(8,128)}, bf16[32,16,256]{2,1,0:T(8,128)(2,1)}) custom-call(bf16[1024,256]{1,0:T(8,128)(2,1)} %bitcast.16, s32[1,512]{1,0:T(1,128)} %bitcast.20, s32[1,512]{1,0:T(1,128)} %bitcast.19, s32[512]{0:T(512)} %res_flat.1, f32[1,256]{1,0:T(1,128)} %bitcast.21, f32[1,256]{1,0:T(1,128)} %bitcast.22, ...), custom_call_target="tpu_custom_call" | custom-call | tf_op jit(solution)/shard_map/pair_backward/pallas_call | solution.py:486
  59.1 2.7 %lay_out.1 = (bf16[1024,256]{1,0:T(8,128)(2,1)}, f32[32,256]{1,0:T(8,128)}, f32[1,32]{1,0:T(1,128)}, f32[32,256]{1,0:T(8,128)}, f32[1,32]{1,0:T(1,128)}, /*index...) custom-call(bf16[1024,256]{1,0:T(8,128)(2,1)} %get-tuple-element.19.ag_any, ...), custom_call_target="tpu_custom_call" | custom-call | tf_op jit(solution)/shard_map/lay_out/pallas_call | solution.py:501

commit v7 on v6

--- a/solution.py
+++ b/solution.py
@@ -255,7 +255,7 @@
         left_sum(lax.rem(q + k, 8))
         lsum_copy(k).start()
 
-    @pl.loop(1, 8)
+    @pl.loop(1, 8, unroll=7)
     def _(k):
         send_left(k)
 
@@ -268,15 +268,13 @@
             product = dot_nt(lb[m * 512 : m * 512 + 512, :], rt[at, :])
             outer[m * 512 : m * 512 + 512, at] = product.astype(BF16)
 
-    wga[...] = jnp.zeros_like(wga)
-
-    @pl.loop(0, 4)
-    def _(t):
-        blocks = [outer[pl.ds(pl.multiple_of((16 * t + e) * 32, 32), 32), :] for e in range(16)]
+    for t in range(2):
+        blocks = [outer[(32 * t + e) * 32 : (32 * t + e) * 32 + 32, :] for e in range(32)]
         rows = [
             jnp.concatenate([block[:, p * 128 : p * 128 + 128] for block in blocks], axis=1) for p in range(16)
         ]
-        wga[...] += dot(jnp.concatenate(rows, axis=0), bd[pl.ds(16 * t, 16)].reshape(2048, 256))
+        part = dot(jnp.concatenate(rows, axis=0), bd[32 * t : 32 * t + 32].reshape(4096, 256))
+        wga[...] = part if t == 0 else wga[...] + part
 
     for t in range(32):
         w1s[t] = wga[t * 16 : t * 16 + 16, :].astype(BF16)
@@ -389,40 +387,58 @@
 
 
 def last_kernel(
-    ag_any, sf_any, wg_any, ag_out, lw_ref, lb_ref, rw_ref, rb_ref, gain_ref, shift_ref, ow_ref, sf, wg, ag, sems
+    ag_any, sf_any, wg_any, ag_out, lw_out, lb_out, rw_out, rb_out, gain_out, shift_out, ow_out,
+    sf, wg, ag, lw, lb, rw, rb, gain, shift, ow, in_sems, out_sems,
 ):
-    moves = [
-        pltpu.make_async_copy(src, dst, sems.at[n])
-        for n, (src, dst) in enumerate(((ag_any, ag), (wg_any, wg), (sf_any, sf), (ag, ag_out)))
+    def load(n, src, dst):
+        return pltpu.make_async_copy(src, dst, in_sems.at[n])
+
+    def store(n, src, dst):
+        return pltpu.make_async_copy(src, dst, out_sems.at[n])
+
+    rows = [pl.ds(n * 256, 256) for n in range(4)]
+    loads = [load(0, wg_any, wg), load(1, sf_any, sf)] + [
+        load(2 + n, ag_any.at[part], ag.at[part]) for n, part in enumerate(rows)
     ]
-    for move in moves[:3]:
+    for move in loads:
         move.start()
-    moves[0].wait()
-    moves[3].start()
-    moves[1].wait()
-    for d in range(32):
-        tile = wg[d // 2 * 2 : d // 2 * 2 + 2, :, d % 2 * 128 : d % 2 * 128 + 128].reshape(32, 128)
-        ow_ref[pl.ds(d, 32, stride=32), :] = tile.astype(F32)
-    moves[2].wait()
+    stores = []
+
+    def send(src, dst):
+        stores.append(store(len(stores), src, dst))
+        stores[-1].start()
+
+    loads[0].wait()
+    for half in range(2):
+        for d in range(32):
+            tile = wg[d // 2 * 2 + half, :, d % 2 * 128 : d % 2 * 128 + 128]
+            ow[pl.ds(half * 512 + d, 16, stride=32), :] = tile.astype(F32)
+        send(ow.at[pl.ds(half * 512, 512)], ow_out.at[pl.ds(half * 512, 512)])
+    loads[1].wait()
     upper = lax.broadcasted_iota(jnp.int32, (8, 128), 0) < 4
     for t in range(16):
         tile = jnp.where(upper, sf[2 * t], sf[2 * t + 1])
-        side, row, lane = (lw_ref, rw_ref)[t // 8], t % 8 // 2 * 8, t % 2 * 128
+        side, row, lane = (lw, rw)[t // 8], t % 8 // 2 * 8, t % 2 * 128
         side[row : row + 8, lane : lane + 128] = tile
-    gain_ref[:, :128] = sf[0, 4:5, :]
-    gain_ref[:, 128:] = sf[1, 0:1, :]
-    shift_ref[:, :128] = sf[2, 4:5, :]
-    shift_ref[:, 128:] = sf[3, 0:1, :]
-    lb_ref[...] = sf[4, 4:5, 0:32]
-    rb_ref[...] = sf[4, 4:5, 32:64]
-    moves[3].wait()
+    gain[:, :128] = sf[0, 4:5, :]
+    gain[:, 128:] = sf[1, 0:1, :]
+    shift[:, :128] = sf[2, 4:5, :]
+    shift[:, 128:] = sf[3, 0:1, :]
+    lb[...] = sf[4, 4:5, 0:32]
+    rb[...] = sf[4, 4:5, 32:64]
+    for src, dst in ((lw, lw_out), (rw, rw_out), (lb, lb_out), (rb, rb_out), (gain, gain_out), (shift, shift_out)):
+        send(src, dst)
+    for n, part in enumerate(rows):
+        loads[2 + n].wait()
+        send(ag.at[part], ag_out.at[part])
+    for move in stores:
+        move.wait()
 
 
 def body(
     alignment, seq_mask, residue_mask, layer_norm_gain, layer_norm_bias, left_projection_weight, left_bias,
     right_projection_weight, right_bias, out_weight, pair_grad,
 ):
-    vmem = pl.BlockSpec(memory_space=pltpu.VMEM)
     hbm = pl.BlockSpec(memory_space=pl.ANY)
     v = pltpu.VMEM
     shape = jax.ShapeDtypeStruct
@@ -505,8 +521,12 @@
             shape((1, 32), F32), shape((1, 256), F32), shape((1, 256), F32), shape((1024, 128), F32),
         ),
         in_specs=[pl.BlockSpec(memory_space=pl.ANY)] * 3,
-        out_specs=(pl.BlockSpec(memory_space=pl.ANY),) + (vmem,) * 7,
-        scratch_shapes=[v((32, 8, 128), F32), v((32, 16, 256), BF16), v((1024, 256), BF16), pltpu.SemaphoreType.DMA((4,))],
+        out_specs=(hbm,) * 8,
+        scratch_shapes=[
+            v((32, 8, 128), F32), v((32, 16, 256), BF16), v((1024, 256), BF16), v((32, 256), F32), v((1, 32), F32),
+            v((32, 256), F32), v((1, 32), F32), v((1, 256), F32), v((1, 256), F32), v((1024, 128), F32),
+            pltpu.SemaphoreType.DMA((6,)), pltpu.SemaphoreType.DMA((12,)),
+        ],
         compiler_params=pltpu.CompilerParams(vmem_limit_bytes=58 * 1024 * 1024),
         name="lay_out",
     )(ag, sf, wg)

time: 61.9 us -> 61.2 us (0.989)
  Pallas kernels: 61.1 us -> 60.4 us
where the time goes in v7:
time: 61.2 us; the launch traced here: 61.1 us
  Pallas kernels  60.4 us (99%)
  between operations  0.65 us (1%)
    pallas_call x1, Pallas kernels, body(): pl.pallas_call(main_kernel, out_shape=(shape((1024, 256), BF16), shape((3...  58 us
    pallas_call x1, Pallas kernels, body(): pl.pallas_call(last_kernel, out_shape=(shape((1024, 256), BF16), shape((3...  2.44 us

profile of v7, /device:TPU:1, one launch (start us, length us, event | category | flops | bytes accessed | tf_op | source)
XLA Modules:
  0.0 61.1 jit_solution(14609820552862564432)
XLA Ops:
  0.6 58.0 %pair_backward.1 = (bf16[1024,256]{1,0:T(8,128)(2,1)}, f32[32,8,128]{2,1,0:T(8,128)}, bf16[32,16,256]{2,1,0:T(8,128)(2,1)}) custom-call(bf16[1024,256]{1,0:T(8,128)(2,1)} %bitcast.16, s32[1,512]{1,0:T(1,128)} %bitcast.20, s32[1,512]{1,0:T(1,128)} %bitcast.19, s32[512]{0:T(512)} %res_flat.1, f32[1,256]{1,0:T(1,128)} %bitcast.21, f32[1,256]{1,0:T(1,128)} %bitcast.22, ...), custom_call_target="tpu_custom_call" | custom-call | tf_op jit(solution)/shard_map/pair_backward/pallas_call | solution.py:502
  58.6 2.4 %lay_out.1 = (bf16[1024,256]{1,0:T(8,128)(2,1)}, f32[32,256]{1,0:T(8,128)}, f32[1,32]{1,0:T(1,128)}, f32[32,256]{1,0:T(8,128)}, f32[1,32]{1,0:T(1,128)}, /*index...) custom-call(bf16[1024,256]{1,0:T(8,128)(2,1)} %get-tuple-element.19.ag_any, ...), custom_call_target="tpu_custom_call" | custom-call | tf_op jit(solution)/shard_map/lay_out/pallas_call | solution.py:517

commit v8 on v7

--- a/solution.py
+++ b/solution.py
@@ -220,6 +220,14 @@
         other_copy(k).wait_recv()
     outer_grads(1 - core)
 
+    arrived(right_copy)
+
+    @pl.loop(0, 16, unroll=4)
+    def _(p):
+        blocks = [rbuf[t, pl.ds(pl.multiple_of(p * 16, 16), 16), :].astype(F32) for t in range(8)]
+        rows = [block[:8] for block in blocks] + [block[8:] for block in blocks]
+        rt[pl.ds(pl.multiple_of(p * 128, 128), 128), :] = jnp.concatenate(rows, axis=0).astype(BF16)
+
     arrived(left_copy)
     for t in range(16):
         block = lb[t * 128 : t * 128 + 128, :].astype(F32)
@@ -239,14 +247,6 @@
         for k in (4, 3, 5, 2, 6, 1, 7):
             rsum_copy(k, part).start()
 
-    arrived(right_copy)
-
-    @pl.loop(0, 16, unroll=4)
-    def _(p):
-        blocks = [rbuf[t, pl.ds(pl.multiple_of(p * 16, 16), 16), :].astype(F32) for t in range(8)]
-        rows = [block[:8] for block in blocks] + [block[8:] for block in blocks]
-        rt[pl.ds(pl.multiple_of(p * 128, 128), 128), :] = jnp.concatenate(rows, axis=0).astype(BF16)
-
     def left_sum(t):
         at = pl.ds(pl.multiple_of(t * 256, 256), 256)
         lss[t] = dot(og[at, :], rt[...]).astype(BF16)
@@ -259,7 +259,6 @@
     def _(k):
         send_left(k)
 
-    left_sum(q)
 
     @pl.loop(0, 8, unroll=4)
     def _(n):
@@ -279,6 +278,7 @@
     for t in range(32):
         w1s[t] = wga[t * 16 : t * 16 + 16, :].astype(BF16)
     scatter_plane(W1, w1s, w1r)
+    left_sum(q)
 
     arrived(lsum_copy)
     total = lss[q].astype(F32)

time: 61.2 us -> 61.3 us (level)
  no operation moved by 1% of the time
where the time goes in v8:
time: 61.3 us; the launch traced here: 61.2 us
  Pallas kernels  60.6 us (99%)
  between operations  0.65 us (1%)
    pallas_call x1, Pallas kernels, body(): pl.pallas_call(main_kernel, out_shape=(shape((1024, 256), BF16), shape((3...  58.1 us
    pallas_call x1, Pallas kernels, body(): pl.pallas_call(last_kernel, out_shape=(shape((1024, 256), BF16), shape((3...  2.44 us

profile of v8, /device:TPU:1, one launch (start us, length us, event | category | flops | bytes accessed | tf_op | source)
XLA Modules:
  0.0 61.2 jit_solution(12313250665148116965)
XLA Ops:
  0.6 58.1 %pair_backward.1 = (bf16[1024,256]{1,0:T(8,128)(2,1)}, f32[32,8,128]{2,1,0:T(8,128)}, bf16[32,16,256]{2,1,0:T(8,128)(2,1)}) custom-call(bf16[1024,256]{1,0:T(8,128)(2,1)} %bitcast.16, s32[1,512]{1,0:T(1,128)} %bitcast.20, s32[1,512]{1,0:T(1,128)} %bitcast.19, s32[512]{0:T(512)} %res_flat.1, f32[1,256]{1,0:T(1,128)} %bitcast.21, f32[1,256]{1,0:T(1,128)} %bitcast.22, ...), custom_call_target="tpu_custom_call" | custom-call | tf_op jit(solution)/shard_map/pair_backward/pallas_call | solution.py:502
  58.8 2.4 %lay_out.1 = (bf16[1024,256]{1,0:T(8,128)(2,1)}, f32[32,256]{1,0:T(8,128)}, f32[1,32]{1,0:T(1,128)}, f32[32,256]{1,0:T(8,128)}, f32[1,32]{1,0:T(1,128)}, /*index...) custom-call(bf16[1024,256]{1,0:T(8,128)(2,1)} %get-tuple-element.19.ag_any, ...), custom_call_target="tpu_custom_call" | custom-call | tf_op jit(solution)/shard_map/lay_out/pallas_call | solution.py:517
